TPU v7x, 256 devices: a whole 4x4x8 slice. The times are simulated.
256 devices in a mesh: row: 16 (over z_hi, y, core), col: 16 (over x, z_lo).
Axes of the slice: x: 4, y: 4, z: 8 (z_hi: 2, z_lo: 4; z = z_hi * 4 + z_lo), core: 2. Of those that a mesh axis runs over, the one named last changes fastest.
Arguments:
- test_grads: bfloat16 [1024, 16384], P('col', 'row'), may hold values from -6 to 6
- inverse_gram: float32 [16384, 16384], P('row', 'col'), may hold values from -0.046875 to 0.046875
- train_grads: bfloat16 [12288, 16384], P('row', 'col'), may hold values from -0.046875 to 0.046875
Outputs:
- scores: float32 [1024, 12288], P('col', 'row')
All inputs are finite; a program needn't handle non-finite values.
Results may differ from a plain program's by a relative error of at most 0.0029.
Values may be sent and summed in bfloat16 or wider, within the bound.
No kernel may reach another device: no remote copies, remote signals or barrier semaphores. Data moves between devices by JAX's collectives and lax.ppermute only.
A program may use at most 64 MiB of HBM per device.

v0:
```python
import jax
import jax.numpy as jnp
from jax import lax
from jax.sharding import PartitionSpec as P


def per_device(test_grads, inverse_gram, train_grads):
    all_tests = lax.all_gather(test_grads, "col", axis=0, tiled=True)
    picked = all_tests.astype(jnp.float32)
    share = lax.psum_scatter(
        jnp.dot(
            picked,
            inverse_gram,
            precision=lax.Precision.HIGHEST,
            preferred_element_type=jnp.float32,
        ),
        "row",
        scatter_dimension=0,
        tiled=True,
    )
    precond_low = lax.all_gather(share.astype(jnp.bfloat16), "row", axis=0, tiled=True)
    picked = precond_low
    return lax.psum_scatter(
        lax.dot_general(
            picked, train_grads, (((1,), (1,)), ((), ())), preferred_element_type=jnp.float32
        ),
        "col",
        scatter_dimension=0,
        tiled=True,
    )


def solution(mesh):
    placed = (P("col", "row"), P("row", "col"), P("row", "col"))
    return jax.shard_map(
        per_device, mesh=mesh, in_specs=placed, out_specs=P("col", "row"), check_vma=False
    )
```

profile of v0, /device:TPU:16, one launch (start us, length us, event | category | flops | bytes accessed | tf_op | source)
XLA Modules:
  0.0 378.6 jit_solution(2639143091276735205)
XLA Ops:
  6.5 0.0 copy-start
  6.5 0.0 all-gather.3.cloned.1.call-start
  6.5 0.7 all-gather.3.cloned.1.call-update
  7.3 0.0 reduce-scatter.3.cloned.1.call-start
  7.3 92.2 %all-gather.3.cloned.1.call-done = bf16[1024,1024]{1,0:T(8,128)(2,1)} async-done(((bf16[64,1024]{1,0:T(8,128)(2,1)}), bf16[1024,1024]{1,0:T(8,128)(2,1)}) %all-gather.3.cloned.1.call-update) | async-done | bytes 2097168 | tf_op jit(solution)/shard_map/all_gather | solution.py:8
  99.5 10.6 %fusion = f32[1024,1024]{1,0:T(8,128)} fusion(bf16[1024,1024]{1,0:T(8,128)(2,1)} %all-gather.3.cloned.1.call-done, f32[1024,1024]{1,0:T(8,128)} %param.4), kind=kOutput, calls=%fused_computation | convolution fusion | flops 12884901888 | bytes 10485760 | tf_op jit(solution)/shard_map/dot_general | solution.py:11
  110.1 0.0 reduce-scatter.3.cloned.1.call-update
  110.2 0.0 all-gather.5.cloned.1.call-start
  110.2 101.6 %reduce-scatter.3.cloned.1.call-done = f32[64,1024]{1,0:T(8,128)} async-done(((f32[1024,1024]{1,0:T(8,128)}), f32[64,1024]{1,0:T(8,128)}) %reduce-scatter.3.cloned.1.call-update) | async-done | bytes 262160 | tf_op jit(solution)/shard_map/reduce_scatter | solution.py:10
  211.8 1.6 convert_element_type.4
  213.4 0.0 all-gather.5.cloned.1.call-update
  213.5 0.0 reduce-scatter.5.cloned.1.call-start
  213.5 60.0 %all-gather.5.cloned.1.call-done = bf16[1024,1024]{1,0:T(8,128)(2,1)} async-done(((bf16[64,1024]{1,0:T(8,128)(2,1)}), bf16[1024,1024]{1,0:T(8,128)(2,1)}) %all-gather.5.cloned.1.call-update) | async-done | bytes 2097168 | tf_op jit(solution)/shard_map/all_gather | solution.py:21
  273.5 0.0 copy-done
  273.5 5.1 %fusion.1 = f32[1024,768]{1,0:T(8,128)} fusion(bf16[1024,1024]{1,0:T(8,128)(2,1)} %all-gather.5.cloned.1.call-done, bf16[768,1024]{1,0:T(8,128)(2,1)S(1)} %copy-done), kind=kOutput, calls=%fused_computation.1 | convolution fusion | flops 1610612736 | bytes 6815744 | tf_op jit(solution)/shard_map/dot_general | solution.py:24
  278.6 0.0 reduce-scatter.5.cloned.1.call-update
  278.6 93.5 %reduce-scatter.5.cloned.1.call-done = f32[64,768]{1,0:T(8,128)} async-done(((f32[1024,768]{1,0:T(8,128)}), f32[64,768]{1,0:T(8,128)}) %reduce-scatter.5.cloned.1.call-update) | async-done | bytes 196624 | tf_op jit(solution)/shard_map/reduce_scatter | solution.py:23
Async XLA Ops:
  6.5 267.0 %copy-start = (bf16[768,1024]{1,0:T(8,128)(2,1)S(1)}, bf16[768,1024]{1,0:T(8,128)(2,1)}, u32[]{:S(2)}) copy-start(bf16[768,1024]{1,0:T(8,128)(2,1)} %param.5) | copy-start | bytes 4718596
  6.5 93.0 %all-gather.3.cloned.1.call-start = ((), (), s32[]{:S(2)}) async-start(), calls=%async_computation.2 | async-start | bytes 2228224 | tf_op jit(solution)/shard_map/all_gather | solution.py:8
  7.3 204.6 %reduce-scatter.3.cloned.1.call-start = ((), (), s32[]{:S(2)}) async-start(), calls=%async_computation.3 | async-start | bytes 4456448 | tf_op jit(solution)/shard_map/reduce_scatter | solution.py:10
  110.2 163.3 %all-gather.5.cloned.1.call-start = ((), (), s32[]{:S(2)}) async-start(), calls=%async_computation.4 | async-start | bytes 2228224 | tf_op jit(solution)/shard_map/all_gather | solution.py:21
  213.5 158.6 %reduce-scatter.5.cloned.1.call-start = ((), (), s32[]{:S(2)}) async-start(), calls=%async_computation.5 | async-start | bytes 3342336 | tf_op jit(solution)/shard_map/reduce_scatter | solution.py:23
Sparse Core Ops, SparseCore 0:
  9.1 90.3 all-gather.2
  110.3 101.4 reduce-scatter.2
  214.9 58.5 all-gather.4
  278.7 93.3 reduce-scatter.4
where the time goes:
time: 379 us
  waiting for transfers between devices  348 us (92%)
  matrix products  15.7 us (4%)
  between operations  13.1 us (3%)
    reduce_scatter x1, waiting for transfers between devices, per_device(): lax.psum_scatter(jnp.dot(picked, inverse_gram, precision=lax.Precision.HI...  102 us
    reduce_scatter x1, waiting for transfers between devices, per_device(): lax.psum_scatter(lax.dot_general(picked, train_grads, (((1,), (1,)), ((),...  93.5 us
    all_gather x1, waiting for transfers between devices, per_device(): all_tests = lax.all_gather(test_grads, 'col', axis=0, tiled=True)  92.2 us
    all_gather x1, waiting for transfers between devices, per_device(): lax.all_gather(share.astype(jnp.bfloat16), 'row', axis=0, tiled=True)  60 us
    dot_general x1, matrix products, per_device(): jnp.dot(picked, inverse_gram, precision=lax.Precision.HIGHEST, preferred_...  10.6 us
  transfers between devices with their start and end apart: 4, of which 4 were waited for; matrix products, arithmetic and copies ran while one was open for 0% of the time, Pallas kernels for 0%

commit v1 on v0

v1 whole, which is shorter than its diff:
```python
import jax
import jax.numpy as jnp
from jax import lax
from jax.experimental import pallas as pl
from jax.experimental.pallas import tpu as pltpu
from jax.sharding import PartitionSpec as P

ZH, Y, CORE, X, ZL = 2, 4, 2, 4, 4
SLOTS = X * ZL
BOTH = ("row", "col")
CROSSED = True
F32, F16, BF16 = jnp.float32, jnp.float16, jnp.bfloat16
VMEM = pl.BlockSpec(memory_space=pltpu.VMEM)
PARAMS = pltpu.CompilerParams(vmem_limit_bytes=48 * 2**20)


def pairs(step):
    def index(zh, y, core, x, zl):
        return ((zh * Y + y) * CORE + core) * (X * ZL) + x * ZL + zl

    return [
        (index(zh, y, core, x, zl), index(*step(zh, y, core, x, zl)))
        for zh in range(ZH)
        for y in range(Y)
        for core in range(CORE)
        for x in range(X)
        for zl in range(ZL)
    ]


TO_CORE = pairs(lambda zh, y, c, x, zl: (zh, y, 1 - c, x, zl))
TO_ZH = pairs(lambda zh, y, c, x, zl: (1 - zh, y, c, x, zl))
TO_Y = [pairs(lambda zh, y, c, x, zl, k=k: (zh, y ^ k, c, x, zl)) for k in range(Y)]
TO_X = [pairs(lambda zh, y, c, x, zl, k=k: (zh, y, c, x ^ k, zl)) for k in range(X)]
TO_ZL = [pairs(lambda zh, y, c, x, zl, k=k: (zh, y, c, x, zl ^ k)) for k in range(ZL)]


def crossed(first):
    def step(zh, y, c, x, zl, k):
        along_x = CROSSED and first == (c == 1) or not CROSSED and not first
        return (zh, y, c, x ^ k, zl) if along_x else (zh, y, c, x, zl ^ k)

    return [pairs(lambda *at, k=k: step(*at, k)) for k in range(4)]


FIRST, SECOND = crossed(True), crossed(False)


def send(value, perm):
    return lax.ppermute(value, BOTH, perm)


def gather(block, perms):
    return jnp.stack([block] + [send(block, perm) for perm in perms[1:]])


def exponent(bound):
    return jnp.clip(15.0 - jnp.ceil(jnp.log2(bound)), -100.0, 100.0)


def pack(values, e):
    head = (values * jnp.exp2(e)).astype(F16)
    return jnp.concatenate([head, jnp.full((8, values.shape[1]), e, F16)])


def unpack(packed):
    e = packed[-1, 0].astype(F32)
    return packed[:-8].astype(F32) * jnp.exp2(-e), e


def scatter_sum(blocks, perms, e):
    total, bound = blocks[0], jnp.exp2(-e)
    for block, perm in zip(blocks[1:], perms[1:]):
        got, its = unpack(send(pack(block, e), perm))
        total, bound = total + got, bound + jnp.exp2(-its)
    return total, -jnp.ceil(jnp.log2(bound))


def split(g):
    high = lax.reduce_precision(g, 8, 7)
    return high.astype(BF16), (g - high).astype(BF16)


def place():
    row = lax.axis_index("row")
    return row % CORE, (row // CORE) % Y


def precond_kernel(tests, near_high, near_low, far_high, far_low, out, top):
    core, y = place()
    rows, width = tests.shape[0], near_high.shape[0]
    group = rows // (SLOTS * Y)
    step = 256

    def body(i, most):
        at = pl.ds(pl.multiple_of(i * step, step), step)
        acc = jnp.dot(tests[:, :width], near_high[:, at], preferred_element_type=F32)
        acc += jnp.dot(tests[:, :width], near_low[:, at], preferred_element_type=F32)
        acc += jnp.dot(tests[:, width:], far_high[:, at], preferred_element_type=F32)
        acc += jnp.dot(tests[:, width:], far_low[:, at], preferred_element_type=F32)
        parts = acc.reshape(4, 4, Y, group, step)
        for second in range(4):
            for first in range(4):
                slot = second * 4 + first
                if CROSSED:
                    slot = jnp.where(core == 0, slot, first * 4 + second)
                for quarter in range(Y):
                    out[quarter ^ y, slot, :, at] = parts[second, first, quarter]
        return jnp.maximum(most, jnp.max(jnp.abs(acc)))

    most = lax.fori_loop(0, near_high.shape[1] // step, body, jnp.float32(0))
    top[...] = jnp.full(top.shape, most)


def scores_kernel(low, near, far, out, top):
    _, y = place()
    group = low.shape[1] // SLOTS
    step = 256
    steps = near.shape[0] // step
    tests = low[...].reshape(-1, low.shape[2])
    most = jnp.float32(0)
    for at_out, trains in ((0, near), (near.shape[0], far)):

        def body(i, most, at_out=at_out, trains=trains):
            rows = pl.ds(pl.multiple_of(i * step, step), step)
            at = pl.ds(pl.multiple_of(at_out + i * step, step), step)
            acc = lax.dot_general(
                tests, trains[rows, :], (((1,), (1,)), ((), ())), preferred_element_type=F32
            )
            parts = acc.reshape(Y, SLOTS, group, step)
            for k in range(Y):
                out[:, k ^ y, :, at] = parts[k]
            return jnp.maximum(most, jnp.max(jnp.abs(acc)))

        most = lax.fori_loop(0, steps, body, most)
    top[...] = jnp.full(top.shape, most)


def call(kernel, shape, args, flops):
    top = jax.ShapeDtypeStruct((8, 128), F32)
    out, top = pl.pallas_call(
        kernel,
        out_shape=(jax.ShapeDtypeStruct(shape, F32), top),
        in_specs=[VMEM] * len(args),
        out_specs=(VMEM, VMEM),
        compiler_params=PARAMS,
        cost_estimate=pl.CostEstimate(flops=flops, bytes_accessed=8 * 2**20, transcendentals=0),
    )(*args)
    return out, exponent(top[0, 0])


def per_device(test_grads, inverse_gram, train_grads):
    core, _ = place()
    tests, width = test_grads.shape
    trains = train_grads.shape[0]
    half = tests // 2
    group = half // Y
    depth = inverse_gram.shape[1]

    mine = jnp.where(core == 0, test_grads[:half], test_grads[half:])
    other = jnp.where(core == 0, test_grads[half:], test_grads[:half])
    block = jnp.concatenate([mine, send(other, TO_CORE)], axis=1)

    near_gram = split(inverse_gram)
    far_gram = split(send(inverse_gram, TO_CORE))
    far_trains = send(train_grads, TO_CORE)

    block = gather(block, FIRST).reshape(4 * half, 2 * width)
    every = gather(block, SECOND).reshape(SLOTS * half, 2 * width)

    part, e = call(
        precond_kernel,
        (Y, SLOTS, group, depth),
        (every, *near_gram, *far_gram),
        8 * SLOTS * half * width * depth,
    )
    part = part.reshape(Y, SLOTS * group, depth)
    total, e = scatter_sum([part[k] for k in range(Y)], TO_Y, e)
    total = total + unpack(send(pack(total, e), TO_ZH))[0]
    low = gather(total.astype(BF16), TO_Y)

    scores, e = call(
        scores_kernel,
        (SLOTS, Y, group, 2 * trains),
        (low, train_grads, far_trains),
        4 * SLOTS * half * trains * depth,
    )
    scores = scores.reshape(X, ZL * half, 2 * trains)
    scores, e = scatter_sum([scores[k] for k in range(X)], TO_X, e)
    scores = scores.reshape(ZL, half, 2 * trains)
    scores, e = scatter_sum([scores[k] for k in range(ZL)], TO_ZL, e)

    kept, sent = scores[:, :trains], scores[:, trains:]
    got = send(sent, TO_CORE)
    return jnp.where(
        core == 0, jnp.concatenate([kept, got]), jnp.concatenate([got, kept])
    )


def solution(mesh):
    placed = (P("col", "row"), P("row", "col"), P("row", "col"))
    return jax.shard_map(
        per_device, mesh=mesh, in_specs=placed, out_specs=P("col", "row"), check_vma=False
    )
```

time: 379 us -> 165 us (0.44)
  the two profiles are of different devices: /device:TPU:16 before, /device:TPU:1 now
where the time goes in v1:
time: 165 us
  waiting for transfers between devices  67.6 us (41%)
  starting transfers between devices  50.3 us (30%)
  Pallas kernels  15.7 us (10%)
  other arithmetic  15.5 us (9%)
  between operations  8.86 us (5%)
  local copies, waits for them, and re-layouts  6.76 us (4%)
    ppermute x23, waiting for transfers between devices, send(): return lax.ppermute(value, BOTH, perm)  67.6 us
    ppermute x23, starting transfers between devices, send(): return lax.ppermute(value, BOTH, perm)  50.3 us
    pallas_call x2, Pallas kernels, call(): pl.pallas_call(kernel, out_shape=(jax.ShapeDtypeStruct(shape, F32), top),...  15.7 us
    convert_element_type x2, other arithmetic, split(): return (high.astype(BF16), (g - high).astype(BF16))  10.3 us
    slice x10, local copies, waits for them, and re-layouts, unpack(): e = packed[-1, 0].astype(F32)  5.26 us
  transfers between devices with their start and end apart: 23, of which 16 were waited for; matrix products, arithmetic and copies ran while one was open for 11% of the time, Pallas kernels for 6%

profile of v1, /device:TPU:1, one launch (start us, length us, event | category | flops | bytes accessed | tf_op | source)
XLA Modules:
  0.0 164.8 jit_solution(10745971624798301474)
XLA Ops:
  0.0 3.2 %collective-permute-start.7 = (f32[1024,1024]{1,0:T(8,128)}, f32[1024,1024]{1,0:T(8,128)}, u32[]{:S(2)}, u32[]{:S(2)}) collective-permute-start(f32[1024,1024]{1,0:T(8,128)} %param.4), channel_id=1, source_target_pairs={{0,16},{1,17},{2,18},{3,19},{4,20},{5,21},{6,22},{7,23},{8,24},{9,... | collective-permute-start | bytes 12582920 | tf_op jit(solution)/shard_map/ppermute | solution.py:50
  4.2 5.9 %collective-permute-done = bf16[32,1024]{1,0:T(8,128)(2,1)S(1)} collective-permute-done((bf16[32,1024]{1,0:T(8,128)(2,1)S(1)}, bf16[32,1024]{1,0:T(8,128)(2,1)S(1)}, u32[]{:S(2)}, u32[]{:S(2)}) %collective-permute-start) | collective-permute-done | bytes 65568 | tf_op jit(solution)/shard_map/ppermute | solution.py:50
  19.1 3.0 %collective-permute-start.5 = (bf16[128,2048]{1,0:T(8,128)(2,1)S(1)}, bf16[128,2048]{1,0:T(8,128)(2,1)S(1)}, u32[]{:S(2)}, u32[]{:S(2)}) collective-permute-start(bf16[128,2048]{1,0:T(8,128)(2,1)S(1)} %bitcast.58), channel_id=1, source_target_pairs={{0,8},{1,9},{2,10},{3,11},{4,12},{5,13},{6,14},{7,15},{8,0},{9,1},... | collective-permute-start | bytes 1572872 | tf_op jit(solution)/shard_map/ppermute | solution.py:50
  22.1 3.7 %collective-permute-start.15 = (bf16[768,1024]{1,0:T(8,128)(2,1)}, bf16[768,1024]{1,0:T(8,128)(2,1)}, u32[]{:S(2)}, u32[]{:S(2)}) collective-permute-start(bf16[768,1024]{1,0:T(8,128)(2,1)} %near.1), channel_id=1, source_target_pairs={{0,16},{1,17},{2,18},{3,19},{4,20},{5,21},{6,22},{7,23},{8,24},{9,... | collective-permute-start | bytes 4718600 | tf_op jit(solution)/shard_map/ppermute | solution.py:50
  25.8 5.1 %fusion = (bf16[1024,1024]{1,0:T(8,128)(2,1)}, bf16[1024,1024]{1,0:T(8,128)(2,1)}) fusion(f32[1024,1024]{1,0:T(8,128)} %param.4), kind=kLoop, calls=%fused_computation.4 | loop fusion | flops 4194304 | bytes 8388608 | tf_op jit(solution)/shard_map/convert_element_type | solution.py:81
  31.5 8.7 %collective-permute-done.5 = bf16[128,2048]{1,0:T(8,128)(2,1)S(1)} collective-permute-done((bf16[128,2048]{1,0:T(8,128)(2,1)S(1)}, bf16[128,2048]{1,0:T(8,128)(2,1)S(1)}, u32[]{:S(2)}, u32[]{:S(2)}) %collective-permute-start.5) | collective-permute-done | bytes 524320 | tf_op jit(solution)/shard_map/ppermute | solution.py:50
  40.5 5.1 %fusion.1 = (bf16[1024,1024]{1,0:T(8,128)(2,1)}, bf16[1024,1024]{1,0:T(8,128)(2,1)}) fusion(f32[1024,1024]{1,0:T(8,128)} %collective-permute-done.7), kind=kLoop, calls=%fused_computation.5 | loop fusion | flops 4194304 | bytes 8388608 | tf_op jit(solution)/shard_map/convert_element_type | solution.py:81
  45.6 9.1 %shard_map.37 = (f32[4,16,8,1024]{3,2,1,0:T(8,128)S(1)}, f32[8,128]{1,0:T(8,128)S(1)}) custom-call(bf16[512,2048]{1,0:T(8,128)(2,1)S(1)} %bitcast.56, bf16[1024,1024]{1,0:T(8,128)(2,1)} %get-tuple-element.16.near_high, bf16[1024,1024]{1,0:T(8,128)(2,1)} %get-tuple-element.15.near_low, bf16[1024,1024]{1,0:T(8,128)(2,1)} %get-tuple-element.14.far_high, ...), custom_call_target="tpu_custom_call" | custom-call | flops 4294967296 | bytes 8388608 | tf_op jit(solution)/shard_map/pallas_call | solution.py:141
  56.2 2.8 %collective-permute-start.10 = (f16[136,1024]{1,0:T(8,128)(2,1)S(1)}, f16[136,1024]{1,0:T(8,128)(2,1)S(1)}, u32[]{:S(2)}, u32[]{:S(2)}) collective-permute-start(f16[136,1024]{1,0:T(8,128)(2,1)S(1)} %concatenate.42), channel_id=1, source_target_pairs={{0,96},{1,97},{2,98},{3,99},{4,100},{5,101},{6,102},{7,103},{8,104... | collective-permute-start | bytes 835592 | tf_op jit(solution)/shard_map/ppermute | solution.py:50
  60.0 10.9 %collective-permute-done.10 = f16[136,1024]{1,0:T(8,128)(2,1)S(1)} collective-permute-done((f16[136,1024]{1,0:T(8,128)(2,1)S(1)}, f16[136,1024]{1,0:T(8,128)(2,1)S(1)}, u32[]{:S(2)}, u32[]{:S(2)}) %collective-permute-start.10) | collective-permute-done | bytes 278560 | tf_op jit(solution)/shard_map/ppermute | solution.py:50
  74.9 5.9 %collective-permute-start.11 = (f16[136,1024]{1,0:T(8,128)(2,1)S(1)}, f16[136,1024]{1,0:T(8,128)(2,1)S(1)}, u32[]{:S(2)}, u32[]{:S(2)}) collective-permute-start(f16[136,1024]{1,0:T(8,128)(2,1)S(1)} %concatenate.43), channel_id=1, source_target_pairs={{0,128},{1,129},{2,130},{3,131},{4,132},{5,133},{6,134},{7,135},{8... | collective-permute-start | bytes 835592 | tf_op jit(solution)/shard_map/ppermute | solution.py:50
  80.8 5.4 %collective-permute-done.11 = f16[136,1024]{1,0:T(8,128)(2,1)S(1)} collective-permute-done((f16[136,1024]{1,0:T(8,128)(2,1)S(1)}, f16[136,1024]{1,0:T(8,128)(2,1)S(1)}, u32[]{:S(2)}, u32[]{:S(2)}) %collective-permute-start.11) | collective-permute-done | bytes 278560 | tf_op jit(solution)/shard_map/ppermute | solution.py:50
  87.8 4.4 %collective-permute-start.13 = (bf16[128,1024]{1,0:T(8,128)(2,1)S(1)}, bf16[128,1024]{1,0:T(8,128)(2,1)S(1)}, u32[]{:S(2)}, u32[]{:S(2)}) collective-permute-start(bf16[128,1024]{1,0:T(8,128)(2,1)S(1)} %add_convert_fusion), channel_id=1, source_target_pairs={{0,64},{1,65},{2,66},{3,67},{4,68},{5,69},{6,70},{7,71},{8,72},{9,... | collective-permute-start | bytes 786440 | tf_op jit(solution)/shard_map/ppermute | solution.py:50
  93.0 9.1 %collective-permute-done.13 = bf16[128,1024]{1,0:T(8,128)(2,1)S(1)} collective-permute-done((bf16[128,1024]{1,0:T(8,128)(2,1)S(1)}, bf16[128,1024]{1,0:T(8,128)(2,1)S(1)}, u32[]{:S(2)}, u32[]{:S(2)}) %collective-permute-start.13) | collective-permute-done | bytes 262176 | tf_op jit(solution)/shard_map/ppermute | solution.py:50
  102.1 3.5 %collective-permute-done.14 = bf16[128,1024]{1,0:T(8,128)(2,1)S(1)} collective-permute-done((bf16[128,1024]{1,0:T(8,128)(2,1)S(1)}, bf16[128,1024]{1,0:T(8,128)(2,1)S(1)}, u32[]{:S(2)}, u32[]{:S(2)}) %collective-permute-start.14) | collective-permute-done | bytes 262176 | tf_op jit(solution)/shard_map/ppermute | solution.py:50
  105.7 6.6 %shard_map.38 = (f32[16,4,8,1536]{3,2,1,0:T(8,128)}, f32[8,128]{1,0:T(8,128)S(1)}) custom-call(bf16[4,128,1024]{2,1,0:T(8,128)(2,1)S(1)} %pad_maximum_fusion.1.low, bf16[768,1024]{1,0:T(8,128)(2,1)S(1)} %copy-done, bf16[768,1024]{1,0:T(8,128)(2,1)} %collective-permute-done.15.far), custom_call_target="tpu_custom_call" | custom-call | flops 1610612736 | bytes 8388608 | tf_op jit(solution)/shard_map/pallas_call | solution.py:141
  113.6 2.1 %multiply_convert_fusion.2 = (f16[4,4,8,1536]{3,2,1,0:T(8,128)(2,1)S(1)}, f16[4,4,8,1536]{3,2,1,0:T(8,128)(2,1)S(1)}, f16[4,4,8,1536]{3,2,1,0:T(8,128)(2,1)S(1)}, f32[4,4,8,1536]{3,2,1,0:T(8,128)S(1)}) fusion(f32[16,4,8,1536]{3,2,1,0:T(8,128)} %get-tuple-element.11, f32[]{:T(128)} %bitcast.26), kind=kLoop, calls=%fused_computation.13 | loop fusion | flops 1179648 | bytes 5111812 | tf_op jit(solution)/shard_map/convert_element_type | solution.py:62
  115.8 4.9 %collective-permute-start.16 = (f16[136,1536]{1,0:T(8,128)(2,1)S(1)}, f16[136,1536]{1,0:T(8,128)(2,1)S(1)}, u32[]{:S(2)}, u32[]{:S(2)}) collective-permute-start(f16[136,1536]{1,0:T(8,128)(2,1)S(1)} %concatenate.44), channel_id=1, source_target_pairs={{0,4},{1,5},{2,6},{3,7},{4,0},{5,1},{6,2},{7,3},{8,12},{9,13},{10,... | collective-permute-start | bytes 1253384 | tf_op jit(solution)/shard_map/ppermute | solution.py:50
  121.3 2.1 %collective-permute-start.18 = (f16[136,1536]{1,0:T(8,128)(2,1)S(1)}, f16[136,1536]{1,0:T(8,128)(2,1)S(1)}, u32[]{:S(2)}, u32[]{:S(2)}) collective-permute-start(f16[136,1536]{1,0:T(8,128)(2,1)S(1)} %concatenate.46), channel_id=1, source_target_pairs={{0,12},{1,13},{2,14},{3,15},{4,8},{5,9},{6,10},{7,11},{8,4},{9,5},... | collective-permute-start | bytes 1253384 | tf_op jit(solution)/shard_map/ppermute | solution.py:50
  123.5 5.1 %collective-permute-done.16 = f16[136,1536]{1,0:T(8,128)(2,1)S(1)} collective-permute-done((f16[136,1536]{1,0:T(8,128)(2,1)S(1)}, f16[136,1536]{1,0:T(8,128)(2,1)S(1)}, u32[]{:S(2)}, u32[]{:S(2)}) %collective-permute-start.16) | collective-permute-done | bytes 417824 | tf_op jit(solution)/shard_map/ppermute | solution.py:50
  129.8 8.2 %collective-permute-done.17 = f16[136,1536]{1,0:T(8,128)(2,1)S(1)} collective-permute-done((f16[136,1536]{1,0:T(8,128)(2,1)S(1)}, f16[136,1536]{1,0:T(8,128)(2,1)S(1)}, u32[]{:S(2)}, u32[]{:S(2)}) %collective-permute-start.17) | collective-permute-done | bytes 417824 | tf_op jit(solution)/shard_map/ppermute | solution.py:50
  142.1 5.0 %collective-permute-start.19 = (f16[40,1536]{1,0:T(8,128)(2,1)S(1)}, f16[40,1536]{1,0:T(8,128)(2,1)S(1)}, u32[]{:S(2)}, u32[]{:S(2)}) collective-permute-start(f16[40,1536]{1,0:T(8,128)(2,1)S(1)} %concatenate.47), channel_id=1, source_target_pairs={{0,1},{1,0},{2,3},{3,2},{4,5},{5,4},{6,7},{7,6},{8,9},{9,8},{10,11... | collective-permute-start | bytes 368648 | tf_op jit(solution)/shard_map/ppermute | solution.py:50
  150.7 3.9 %collective-permute-done.20 = f16[40,1536]{1,0:T(8,128)(2,1)S(1)} collective-permute-done((f16[40,1536]{1,0:T(8,128)(2,1)S(1)}, f16[40,1536]{1,0:T(8,128)(2,1)S(1)}, u32[]{:S(2)}, u32[]{:S(2)}) %collective-permute-start.20) | collective-permute-done | bytes 122912 | tf_op jit(solution)/shard_map/ppermute | solution.py:50
  157.1 6.0 %collective-permute-start.22 = (f32[32,768]{1,0:T(8,128)S(1)}, f32[32,768]{1,0:T(8,128)S(1)}, u32[]{:S(2)}, u32[]{:S(2)}) collective-permute-start(f32[32,768]{1,0:T(8,128)S(1)} %get-tuple-element.28), channel_id=1, source_target_pairs={{0,16},{1,17},{2,18},{3,19},{4,20},{5,21},{6,22},{7,23},{8,24},{9,... | collective-permute-start | bytes 294920 | tf_op jit(solution)/shard_map/ppermute | solution.py:50
  (64 shorter events, 26.0 us)
Async XLA Ops:
  0.0 40.5 %collective-permute-start.7 = (f32[1024,1024]{1,0:T(8,128)}, f32[1024,1024]{1,0:T(8,128)}, u32[]{:S(2)}, u32[]{:S(2)}) collective-permute-start(f32[1024,1024]{1,0:T(8,128)} %param.4), channel_id=1, source_target_pairs={{0,16},{1,17},{2,18},{3,19},{4,20},{5,21},{6,22},{7,23},{8,24},{9,... | collective-permute-start | bytes 12582920 | tf_op jit(solution)/shard_map/ppermute | solution.py:50
  4.1 6.0 %collective-permute-start = (bf16[32,1024]{1,0:T(8,128)(2,1)S(1)}, bf16[32,1024]{1,0:T(8,128)(2,1)S(1)}, u32[]{:S(2)}, u32[]{:S(2)}) collective-permute-start(bf16[32,1024]{1,0:T(8,128)(2,1)S(1)} %get-tuple-element.32), channel_id=1, source_target_pairs={{0,16},{1,17},{2,18},{3,19},{4,20},{5,21},{6,22},{7,23},{8,24},{9,... | collective-permute-start | bytes 196616 | tf_op jit(solution)/shard_map/ppermute | solution.py:50
  10.1 4.2 %collective-permute-start.1 = (bf16[32,2048]{1,0:T(8,128)(2,1)S(1)}, bf16[32,2048]{1,0:T(8,128)(2,1)S(1)}, u32[]{:S(2)}, u32[]{:S(2)}) collective-permute-start(bf16[32,2048]{1,0:T(8,128)(2,1)S(1)} %get-tuple-element.30), channel_id=1, source_target_pairs={{0,1},{1,0},{2,3},{3,2},{4,5},{5,4},{6,7},{7,6},{8,9},{9,8},{10,11... | collective-permute-start | bytes 393224 | tf_op jit(solution)/shard_map/ppermute | solution.py:50
  10.2 5.7 %collective-permute-start.2 = (bf16[32,2048]{1,0:T(8,128)(2,1)S(1)}, bf16[32,2048]{1,0:T(8,128)(2,1)S(1)}, u32[]{:S(2)}, u32[]{:S(2)}) collective-permute-start(bf16[32,2048]{1,0:T(8,128)(2,1)S(1)} %get-tuple-element.30), channel_id=1, source_target_pairs={{0,2},{1,3},{2,0},{3,1},{4,6},{5,7},{6,4},{7,5},{8,10},{9,11},{10,... | collective-permute-start | bytes 393224 | tf_op jit(solution)/shard_map/ppermute | solution.py:50
  12.2 5.3 %collective-permute-start.3 = (bf16[32,2048]{1,0:T(8,128)(2,1)S(1)}, bf16[32,2048]{1,0:T(8,128)(2,1)S(1)}, u32[]{:S(2)}, u32[]{:S(2)}) collective-permute-start(bf16[32,2048]{1,0:T(8,128)(2,1)S(1)} %get-tuple-element.30), channel_id=1, source_target_pairs={{0,3},{1,2},{2,1},{3,0},{4,7},{5,6},{6,5},{7,4},{8,11},{9,10},{10,... | collective-permute-start | bytes 393224 | tf_op jit(solution)/shard_map/ppermute | solution.py:50
  17.5 14.0 %collective-permute-start.4 = (bf16[128,2048]{1,0:T(8,128)(2,1)S(1)}, bf16[128,2048]{1,0:T(8,128)(2,1)S(1)}, u32[]{:S(2)}, u32[]{:S(2)}) collective-permute-start(bf16[128,2048]{1,0:T(8,128)(2,1)S(1)} %bitcast.57), channel_id=1, source_target_pairs={{0,4},{1,5},{2,6},{3,7},{4,0},{5,1},{6,2},{7,3},{8,12},{9,13},{10,... | collective-permute-start | bytes 1572872 | tf_op jit(solution)/shard_map/ppermute | solution.py:50
  19.1 21.1 %collective-permute-start.5 = (bf16[128,2048]{1,0:T(8,128)(2,1)S(1)}, bf16[128,2048]{1,0:T(8,128)(2,1)S(1)}, u32[]{:S(2)}, u32[]{:S(2)}) collective-permute-start(bf16[128,2048]{1,0:T(8,128)(2,1)S(1)} %bitcast.58), channel_id=1, source_target_pairs={{0,8},{1,9},{2,10},{3,11},{4,12},{5,13},{6,14},{7,15},{8,0},{9,1},... | collective-permute-start | bytes 1572872 | tf_op jit(solution)/shard_map/ppermute | solution.py:50
  22.1 18.1 %collective-permute-start.6 = (bf16[128,2048]{1,0:T(8,128)(2,1)S(1)}, bf16[128,2048]{1,0:T(8,128)(2,1)S(1)}, u32[]{:S(2)}, u32[]{:S(2)}) collective-permute-start(bf16[128,2048]{1,0:T(8,128)(2,1)S(1)} %bitcast.59), channel_id=1, source_target_pairs={{0,12},{1,13},{2,14},{3,15},{4,8},{5,9},{6,10},{7,11},{8,4},{9,5},... | collective-permute-start | bytes 1572872 | tf_op jit(solution)/shard_map/ppermute | solution.py:50
  22.1 83.6 %collective-permute-start.15 = (bf16[768,1024]{1,0:T(8,128)(2,1)}, bf16[768,1024]{1,0:T(8,128)(2,1)}, u32[]{:S(2)}, u32[]{:S(2)}) collective-permute-start(bf16[768,1024]{1,0:T(8,128)(2,1)} %near.1), channel_id=1, source_target_pairs={{0,16},{1,17},{2,18},{3,19},{4,20},{5,21},{6,22},{7,23},{8,24},{9,... | collective-permute-start | bytes 4718600 | tf_op jit(solution)/shard_map/ppermute | solution.py:50
  56.2 14.6 %collective-permute-start.10 = (f16[136,1024]{1,0:T(8,128)(2,1)S(1)}, f16[136,1024]{1,0:T(8,128)(2,1)S(1)}, u32[]{:S(2)}, u32[]{:S(2)}) collective-permute-start(f16[136,1024]{1,0:T(8,128)(2,1)S(1)} %concatenate.42), channel_id=1, source_target_pairs={{0,96},{1,97},{2,98},{3,99},{4,100},{5,101},{6,102},{7,103},{8,104... | collective-permute-start | bytes 835592 | tf_op jit(solution)/shard_map/ppermute | solution.py:50
  59.1 13.0 %collective-permute-start.9 = (f16[136,1024]{1,0:T(8,128)(2,1)S(1)}, f16[136,1024]{1,0:T(8,128)(2,1)S(1)}, u32[]{:S(2)}, u32[]{:S(2)}) collective-permute-start(f16[136,1024]{1,0:T(8,128)(2,1)S(1)} %concatenate.41), channel_id=1, source_target_pairs={{0,64},{1,65},{2,66},{3,67},{4,68},{5,69},{6,70},{7,71},{8,72},{9,... | collective-permute-start | bytes 835592 | tf_op jit(solution)/shard_map/ppermute | solution.py:50
  59.6 13.8 %collective-permute-start.8 = (f16[136,1024]{1,0:T(8,128)(2,1)S(1)}, f16[136,1024]{1,0:T(8,128)(2,1)S(1)}, u32[]{:S(2)}, u32[]{:S(2)}) collective-permute-start(f16[136,1024]{1,0:T(8,128)(2,1)S(1)} %concatenate.40), channel_id=1, source_target_pairs={{0,32},{1,33},{2,34},{3,35},{4,36},{5,37},{6,38},{7,39},{8,40},{9,... | collective-permute-start | bytes 835592 | tf_op jit(solution)/shard_map/ppermute | solution.py:50
  74.9 30.8 %copy-start = (bf16[768,1024]{1,0:T(8,128)(2,1)S(1)}, bf16[768,1024]{1,0:T(8,128)(2,1)}, u32[]{:S(2)}) copy-start(bf16[768,1024]{1,0:T(8,128)(2,1)} %near.1) | copy-start | bytes 4718596
  74.9 11.3 %collective-permute-start.11 = (f16[136,1024]{1,0:T(8,128)(2,1)S(1)}, f16[136,1024]{1,0:T(8,128)(2,1)S(1)}, u32[]{:S(2)}, u32[]{:S(2)}) collective-permute-start(f16[136,1024]{1,0:T(8,128)(2,1)S(1)} %concatenate.43), channel_id=1, source_target_pairs={{0,128},{1,129},{2,130},{3,131},{4,132},{5,133},{6,134},{7,135},{8... | collective-permute-start | bytes 835592 | tf_op jit(solution)/shard_map/ppermute | solution.py:50
  87.7 5.3 %collective-permute-start.12 = (bf16[128,1024]{1,0:T(8,128)(2,1)S(1)}, bf16[128,1024]{1,0:T(8,128)(2,1)S(1)}, u32[]{:S(2)}, u32[]{:S(2)}) collective-permute-start(bf16[128,1024]{1,0:T(8,128)(2,1)S(1)} %add_convert_fusion), channel_id=1, source_target_pairs={{0,32},{1,33},{2,34},{3,35},{4,36},{5,37},{6,38},{7,39},{8,40},{9,... | collective-permute-start | bytes 786440 | tf_op jit(solution)/shard_map/ppermute | solution.py:50
  87.8 14.3 %collective-permute-start.13 = (bf16[128,1024]{1,0:T(8,128)(2,1)S(1)}, bf16[128,1024]{1,0:T(8,128)(2,1)S(1)}, u32[]{:S(2)}, u32[]{:S(2)}) collective-permute-start(bf16[128,1024]{1,0:T(8,128)(2,1)S(1)} %add_convert_fusion), channel_id=1, source_target_pairs={{0,64},{1,65},{2,66},{3,67},{4,68},{5,69},{6,70},{7,71},{8,72},{9,... | collective-permute-start | bytes 786440 | tf_op jit(solution)/shard_map/ppermute | solution.py:50
  92.2 13.4 %collective-permute-start.14 = (bf16[128,1024]{1,0:T(8,128)(2,1)S(1)}, bf16[128,1024]{1,0:T(8,128)(2,1)S(1)}, u32[]{:S(2)}, u32[]{:S(2)}) collective-permute-start(bf16[128,1024]{1,0:T(8,128)(2,1)S(1)} %add_convert_fusion), channel_id=1, source_target_pairs={{0,96},{1,97},{2,98},{3,99},{4,100},{5,101},{6,102},{7,103},{8,104... | collective-permute-start | bytes 786440 | tf_op jit(solution)/shard_map/ppermute | solution.py:50
  115.8 12.8 %collective-permute-start.16 = (f16[136,1536]{1,0:T(8,128)(2,1)S(1)}, f16[136,1536]{1,0:T(8,128)(2,1)S(1)}, u32[]{:S(2)}, u32[]{:S(2)}) collective-permute-start(f16[136,1536]{1,0:T(8,128)(2,1)S(1)} %concatenate.44), channel_id=1, source_target_pairs={{0,4},{1,5},{2,6},{3,7},{4,0},{5,1},{6,2},{7,3},{8,12},{9,13},{10,... | collective-permute-start | bytes 1253384 | tf_op jit(solution)/shard_map/ppermute | solution.py:50
  120.8 17.2 %collective-permute-start.17 = (f16[136,1536]{1,0:T(8,128)(2,1)S(1)}, f16[136,1536]{1,0:T(8,128)(2,1)S(1)}, u32[]{:S(2)}, u32[]{:S(2)}) collective-permute-start(f16[136,1536]{1,0:T(8,128)(2,1)S(1)} %concatenate.45), channel_id=1, source_target_pairs={{0,8},{1,9},{2,10},{3,11},{4,12},{5,13},{6,14},{7,15},{8,0},{9,1},... | collective-permute-start | bytes 1253384 | tf_op jit(solution)/shard_map/ppermute | solution.py:50
  121.3 19.1 %collective-permute-start.18 = (f16[136,1536]{1,0:T(8,128)(2,1)S(1)}, f16[136,1536]{1,0:T(8,128)(2,1)S(1)}, u32[]{:S(2)}, u32[]{:S(2)}) collective-permute-start(f16[136,1536]{1,0:T(8,128)(2,1)S(1)} %concatenate.46), channel_id=1, source_target_pairs={{0,12},{1,13},{2,14},{3,15},{4,8},{5,9},{6,10},{7,11},{8,4},{9,5},... | collective-permute-start | bytes 1253384 | tf_op jit(solution)/shard_map/ppermute | solution.py:50
  142.1 7.4 %collective-permute-start.19 = (f16[40,1536]{1,0:T(8,128)(2,1)S(1)}, f16[40,1536]{1,0:T(8,128)(2,1)S(1)}, u32[]{:S(2)}, u32[]{:S(2)}) collective-permute-start(f16[40,1536]{1,0:T(8,128)(2,1)S(1)} %concatenate.47), channel_id=1, source_target_pairs={{0,1},{1,0},{2,3},{3,2},{4,5},{5,4},{6,7},{7,6},{8,9},{9,8},{10,11... | collective-permute-start | bytes 368648 | tf_op jit(solution)/shard_map/ppermute | solution.py:50
  147.1 7.5 %collective-permute-start.20 = (f16[40,1536]{1,0:T(8,128)(2,1)S(1)}, f16[40,1536]{1,0:T(8,128)(2,1)S(1)}, u32[]{:S(2)}, u32[]{:S(2)}) collective-permute-start(f16[40,1536]{1,0:T(8,128)(2,1)S(1)} %concatenate.48), channel_id=1, source_target_pairs={{0,2},{1,3},{2,0},{3,1},{4,6},{5,7},{6,4},{7,5},{8,10},{9,11},{10,... | collective-permute-start | bytes 368648 | tf_op jit(solution)/shard_map/ppermute | solution.py:50
  147.7 8.2 %collective-permute-start.21 = (f16[40,1536]{1,0:T(8,128)(2,1)S(1)}, f16[40,1536]{1,0:T(8,128)(2,1)S(1)}, u32[]{:S(2)}, u32[]{:S(2)}) collective-permute-start(f16[40,1536]{1,0:T(8,128)(2,1)S(1)} %concatenate.49), channel_id=1, source_target_pairs={{0,3},{1,2},{2,1},{3,0},{4,7},{5,6},{6,5},{7,4},{8,11},{9,10},{10,... | collective-permute-start | bytes 368648 | tf_op jit(solution)/shard_map/ppermute | solution.py:50
  157.1 6.9 %collective-permute-start.22 = (f32[32,768]{1,0:T(8,128)S(1)}, f32[32,768]{1,0:T(8,128)S(1)}, u32[]{:S(2)}, u32[]{:S(2)}) collective-permute-start(f32[32,768]{1,0:T(8,128)S(1)} %get-tuple-element.28), channel_id=1, source_target_pairs={{0,16},{1,17},{2,18},{3,19},{4,20},{5,21},{6,22},{7,23},{8,24},{9,... | collective-permute-start | bytes 294920 | tf_op jit(solution)/shard_map/ppermute | solution.py:50

commit v2 on v0

v2 whole, which is shorter than its diff:
```python
import jax
import jax.numpy as jnp
from jax import lax
from jax.experimental import pallas as pl
from jax.experimental.pallas import tpu as pltpu
from jax.sharding import PartitionSpec as P

ZH, Y, CORE, X, ZL = 2, 4, 2, 4, 4
BOTH = ("row", "col")
F32, F16, BF16 = jnp.float32, jnp.float16, jnp.bfloat16
VMEM = pl.BlockSpec(memory_space=pltpu.VMEM)
PARAMS = pltpu.CompilerParams(vmem_limit_bytes=24 * 2**20)


def pairs(step):
    def index(zh, y, core, x, zl):
        return ((zh * Y + y) * CORE + core) * (X * ZL) + x * ZL + zl

    return [
        (index(zh, y, core, x, zl), index(*step(zh, y, core, x, zl)))
        for zh in range(ZH)
        for y in range(Y)
        for core in range(CORE)
        for x in range(X)
        for zl in range(ZL)
    ]


TO_CORE = pairs(lambda zh, y, c, x, zl: (zh, y, 1 - c, x, zl))
TO_ZH = pairs(lambda zh, y, c, x, zl: (1 - zh, y, c, x, zl))
TO_Y = [pairs(lambda zh, y, c, x, zl, k=k: (zh, y ^ k, c, x, zl)) for k in range(Y)]


def crossed(first):
    def step(zh, y, c, x, zl, k):
        along_x = first == (c == 1)
        return (zh, y, c, x ^ k, zl) if along_x else (zh, y, c, x, zl ^ k)

    return [pairs(lambda *at, k=k: step(*at, k)) for k in range(4)]


FIRST, SECOND = crossed(True), crossed(False)


def send(value, perm):
    return lax.ppermute(value, BOTH, perm)


def gather(block, perms):
    return jnp.stack([block] + [send(block, perm) for perm in perms[1:]])


def pack(values, e):
    head = (values * jnp.exp2(e)).astype(F16)
    tail = jnp.broadcast_to(e, (8, values.shape[1])).astype(F16)
    return jnp.concatenate([head, tail])


def unpack(packed):
    e = packed[-1:].astype(F32)
    return packed[:-8].astype(F32) * jnp.exp2(-e), e


def scatter_sum(blocks, perms, e):
    total, least = blocks[0], e
    sent = [send(pack(block, e), perm) for block, perm in zip(blocks[1:], perms[1:])]
    for packed in sent:
        got, its = unpack(packed)
        total, least = total + got, jnp.minimum(least, its)
    return total, least - 2.0


def y_place():
    return (lax.axis_index("row") // CORE) % Y


def note_top(i, acc, most, top):
    @pl.when(i == 0)
    def _():
        most[...] = jnp.zeros(most.shape, F32)

    most[...] = jnp.maximum(most[...], jnp.max(jnp.abs(acc).reshape(-1, 8, acc.shape[1]), axis=0))

    @pl.when(i == pl.num_programs(0) - 1)
    def _():
        bound = jnp.broadcast_to(jnp.max(most[...]), top.shape)
        top[...] = jnp.clip(15.0 - jnp.ceil(jnp.log2(bound)), -100.0, 100.0)


def precond_kernel(tests, near, far, out, top, most):
    i, y = pl.program_id(0), y_place()
    rows, width = tests.shape[0], near.shape[0]
    acc = None
    for at, gram in ((0, near), (width, far)):
        high = gram[...].astype(BF16)
        low = (gram[...] - high.astype(F32)).astype(BF16)
        for part in (high, low):
            new = jnp.dot(tests[:, at : at + width], part, preferred_element_type=F32)
            acc = new if acc is None else acc + new
    parts = acc.reshape(out.shape[1], Y, out.shape[2], -1)
    for quarter in range(Y):
        out[quarter ^ y] = parts[:, quarter]
    note_top(i, acc, most, top)


def scores_kernel(low, near, far, out, top, most):
    i, y = pl.program_id(0), y_place()
    tests = low[...].reshape(-1, low.shape[2])

    def product(trains):
        acc = lax.dot_general(
            tests, trains[...], (((1,), (1,)), ((), ())), preferred_element_type=F32
        )
        parts = acc.reshape(Y, out.shape[0], out.shape[2], -1)
        for k in range(Y):
            out[:, k ^ y] = parts[k]
        note_top(i, acc, most, top)

    pl.when(i < pl.num_programs(0) // 2)(lambda: product(near))
    pl.when(i >= pl.num_programs(0) // 2)(lambda: product(far))


def precond(tests, near, far):
    rows, (width, depth) = tests.shape[0], near.shape
    slots, group, step = rows // 32, 8, 256
    block = pl.BlockSpec((width, step), lambda i: (0, i))
    return pl.pallas_call(
        precond_kernel,
        grid=(depth // step,),
        in_specs=[VMEM, block, block],
        out_specs=(pl.BlockSpec((Y, slots, group, step), lambda i: (0, 0, 0, i)), pl.BlockSpec((8, depth), lambda i: (0, 0))),
        out_shape=(jax.ShapeDtypeStruct((Y, slots, group, depth), F32), jax.ShapeDtypeStruct((8, depth), F32)),
        scratch_shapes=[pltpu.VMEM((8, step), F32)],
        compiler_params=PARAMS,
        cost_estimate=pl.CostEstimate(flops=8 * rows * width * depth, bytes_accessed=2**23, transcendentals=0),
        name="precond",
    )(tests, near, far)


def scores_of(low, near, far):
    trains, depth = near.shape
    slots, group, step = low.shape[1] // 8, 8, 256
    n = trains // step
    return pl.pallas_call(
        scores_kernel,
        grid=(2 * n,),
        in_specs=[
            VMEM,
            pl.BlockSpec((step, depth), lambda i: (jnp.minimum(i, n - 1), 0)),
            pl.BlockSpec((step, depth), lambda i: (jnp.maximum(i - n, 0), 0)),
        ],
        out_specs=(pl.BlockSpec((slots, Y, group, step), lambda i: (0, 0, 0, i)), pl.BlockSpec((8, 2 * trains), lambda i: (0, 0))),
        out_shape=(jax.ShapeDtypeStruct((slots, Y, group, 2 * trains), F32), jax.ShapeDtypeStruct((8, 2 * trains), F32)),
        scratch_shapes=[pltpu.VMEM((8, step), F32)],
        compiler_params=PARAMS,
        cost_estimate=pl.CostEstimate(flops=4 * low.shape[0] * low.shape[1] * trains * depth, bytes_accessed=2**22, transcendentals=0),
        name="scores",
    )(low, near, far)


def per_device(test_grads, inverse_gram, train_grads):
    core = lax.axis_index("row") % CORE
    tests, width = test_grads.shape
    trains = train_grads.shape[0]
    half = tests // 2

    mine = jnp.where(core == 0, test_grads[:half], test_grads[half:])
    other = jnp.where(core == 0, test_grads[half:], test_grads[:half])
    got = send(other, TO_CORE)
    got, inverse_gram, train_grads = lax.optimization_barrier((got, inverse_gram, train_grads))
    far_gram = send(inverse_gram, TO_CORE)
    far_trains = send(train_grads, TO_CORE)

    block = jnp.concatenate([mine, got], axis=1)
    block = gather(block, FIRST).reshape(4 * half, 2 * width)
    slot1, slot3 = send(block, SECOND[1]), send(block, SECOND[3])
    part = precond(jnp.concatenate([block, slot1]), inverse_gram, far_gram)
    slot3, part = lax.optimization_barrier((slot3, part))
    slot2 = send(slot3, SECOND[1])

    def summed(part, e):
        part = part.reshape(Y, -1, part.shape[3])
        return scatter_sum([part[k] for k in range(Y)], TO_Y, e[:1])

    def rounded(total, e):
        return (total + unpack(send(pack(total, e), TO_ZH))[0]).astype(BF16)

    def product(low):
        scores, e = scores_of(low, train_grads, far_trains)
        scores = scores.reshape(2, 4 * half, 2 * trains)
        return [(scores[j], e[:1]) for j in range(2)]

    first = summed(*part)
    part = precond(jnp.concatenate([slot2, slot3]), inverse_gram, far_gram)
    first, part = lax.optimization_barrier((first, part))
    second = summed(*part)
    low0 = rounded(*first)
    low1 = rounded(*second)
    low0 = gather(low0, TO_Y)
    low1 = gather(low1, TO_Y)
    block0, block1 = product(low0)
    block2, block3 = product(low1)
    total, least = block0
    for (block, e), k in ((block1, 1), (block2, 2), (block3, 3)):
        got, its = unpack(send(pack(block, e), SECOND[k]))
        total, least = total + got, jnp.minimum(least, its)
    total = total.reshape(4, half, 2 * trains)
    total, _ = scatter_sum([total[k] for k in range(4)], FIRST, least - 2.0)

    kept, sent = total[:, :trains], total[:, trains:]
    got = send(sent, TO_CORE)
    return jnp.where(
        core == 0, jnp.concatenate([kept, got]), jnp.concatenate([got, kept])
    )


def solution(mesh):
    placed = (P("col", "row"), P("row", "col"), P("row", "col"))
    return jax.shard_map(
        per_device, mesh=mesh, in_specs=placed, out_specs=P("col", "row"), check_vma=False
    )
```

time: 379 us -> 118 us (0.31)
  the two profiles are of different devices: /device:TPU:16 before, /device:TPU:1 now
where the time goes in v2:
time: 118 us
  starting transfers between devices  50.1 us (42%)
  waiting for transfers between devices  47 us (40%)
  Pallas kernels  13 us (11%)
  other arithmetic  4.41 us (4%)
  local copies, waits for them, and re-layouts  2.54 us (2%)
    ppermute x30, starting transfers between devices, send(): return lax.ppermute(value, BOTH, perm)  50.1 us
    ppermute x30, waiting for transfers between devices, send(): return lax.ppermute(value, BOTH, perm)  47 us
    pallas_call x2, Pallas kernels, precond(): pl.pallas_call(precond_kernel, grid=(depth // step,), in_specs=[VMEM, blo...  7.81 us
    pallas_call x2, Pallas kernels, scores_of(): pl.pallas_call(scores_kernel, grid=(2 * n,), in_specs=[VMEM, pl.BlockSpec...  5.23 us
  transfers between devices with their start and end apart: 30, of which 18 were waited for; matrix products, arithmetic and copies ran while one was open for 2% of the time, Pallas kernels for 11%

profile of v2, /device:TPU:1, one launch (start us, length us, event | category | flops | bytes accessed | tf_op | source)
XLA Modules:
  0.0 117.5 jit_solution(14466281759102572182)
XLA Ops:
  0.9 3.3 %collective-permute-start = (bf16[32,1024]{1,0:T(8,128)(2,1)S(1)}, bf16[32,1024]{1,0:T(8,128)(2,1)S(1)}, u32[]{:S(2)}, u32[]{:S(2)}) collective-permute-start(bf16[32,1024]{1,0:T(8,128)(2,1)S(1)} %get-tuple-element.73), channel_id=1, source_target_pairs={{0,16},{1,17},{2,18},{3,19},{4,20},{5,21},{6,22},{7,23},{8,24},{9,... | collective-permute-start | bytes 196616 | tf_op jit(solution)/shard_map/ppermute | solution.py:46
  8.8 3.3 %collective-permute-done.3 = bf16[32,2048]{1,0:T(8,128)(2,1)S(1)} collective-permute-done((bf16[32,2048]{1,0:T(8,128)(2,1)S(1)}, bf16[32,2048]{1,0:T(8,128)(2,1)S(1)}, u32[]{:S(2)}, u32[]{:S(2)}) %collective-permute-start.3) | collective-permute-done | bytes 131104 | tf_op jit(solution)/shard_map/ppermute | solution.py:46
  13.4 2.8 %collective-permute-start.4 = (bf16[128,2048]{1,0:T(8,128)(2,1)S(1)}, bf16[128,2048]{1,0:T(8,128)(2,1)S(1)}, u32[]{:S(2)}, u32[]{:S(2)}) collective-permute-start(bf16[128,2048]{1,0:T(8,128)(2,1)S(1)} %bitcast.85), channel_id=1, source_target_pairs={{0,12},{1,13},{2,14},{3,15},{4,8},{5,9},{6,10},{7,11},{8,4},{9,5},... | collective-permute-start | bytes 1572872 | tf_op jit(solution)/shard_map/ppermute | solution.py:46
  16.3 5.1 %collective-permute-done.5 = bf16[128,2048]{1,0:T(8,128)(2,1)S(1)} collective-permute-done((bf16[128,2048]{1,0:T(8,128)(2,1)S(1)}, bf16[128,2048]{1,0:T(8,128)(2,1)S(1)}, u32[]{:S(2)}, u32[]{:S(2)}) %collective-permute-start.5) | collective-permute-done | bytes 524320 | tf_op jit(solution)/shard_map/ppermute | solution.py:46
  21.5 2.2 %copy-done = f32[1024,1024]{1,0:T(8,128)S(1)} copy-done((f32[1024,1024]{1,0:T(8,128)S(1)}, f32[1024,1024]{1,0:T(8,128)}, u32[]{:S(2)}) %copy-start) | copy-done | bytes 4194328
  23.7 3.9 %precond.2 = (f32[4,8,8,1024]{3,2,1,0:T(8,128)S(1)}, f32[8,1024]{1,0:T(8,128)S(1)}) custom-call(bf16[256,2048]{1,0:T(8,128)(2,1)S(1)} %pad_maximum_fusion.tests, f32[1024,1024]{1,0:T(8,128)S(1)} %copy-done, f32[1024,1024]{1,0:T(8,128)S(1)} %collective-permute-done.6.far), custom_call_target="tpu_custom_call" | custom-call | flops 2147483648 | bytes 8388608 | tf_op jit(solution)/shard_map/precond/pallas_call | solution.py:127
  28.7 2.8 %collective-permute-start.9 = (f16[72,1024]{1,0:T(8,128)(2,1)S(1)}, f16[72,1024]{1,0:T(8,128)(2,1)S(1)}, u32[]{:S(2)}, u32[]{:S(2)}) collective-permute-start(f16[72,1024]{1,0:T(8,128)(2,1)S(1)} %get-tuple-element.84), channel_id=1, source_target_pairs={{0,96},{1,97},{2,98},{3,99},{4,100},{5,101},{6,102},{7,103},{8,104... | collective-permute-start | bytes 442376 | tf_op jit(solution)/shard_map/ppermute | solution.py:46
  32.7 4.1 %collective-permute-start.15 = (bf16[768,1024]{1,0:T(8,128)(2,1)S(1)}, bf16[768,1024]{1,0:T(8,128)(2,1)S(1)}, u32[]{:S(2)}, u32[]{:S(2)}) collective-permute-start(bf16[768,1024]{1,0:T(8,128)(2,1)S(1)} %copy-done.1), channel_id=1, source_target_pairs={{0,16},{1,17},{2,18},{3,19},{4,20},{5,21},{6,22},{7,23},{8,24},{9,... | collective-permute-start | bytes 4718600 | tf_op jit(solution)/shard_map/ppermute | solution.py:46
  37.3 3.3 %collective-permute-done.10 = bf16[128,2048]{1,0:T(8,128)(2,1)S(1)} collective-permute-done((bf16[128,2048]{1,0:T(8,128)(2,1)S(1)}, bf16[128,2048]{1,0:T(8,128)(2,1)S(1)}, u32[]{:S(2)}, u32[]{:S(2)}) %collective-permute-start.10) | collective-permute-done | bytes 524320 | tf_op jit(solution)/shard_map/ppermute | solution.py:46
  40.6 3.9 %precond.3 = (f32[4,8,8,1024]{3,2,1,0:T(8,128)S(1)}, f32[8,1024]{1,0:T(8,128)S(1)}) custom-call(bf16[256,2048]{1,0:T(8,128)(2,1)S(1)} %pad_maximum_fusion.1.tests, f32[1024,1024]{1,0:T(8,128)S(1)} %copy-done, f32[1024,1024]{1,0:T(8,128)S(1)} %collective-permute-done.6.far), custom_call_target="tpu_custom_call" | custom-call | flops 2147483648 | bytes 8388608 | tf_op jit(solution)/shard_map/precond/pallas_call | solution.py:127
  44.7 5.0 %collective-permute-start.11 = (f16[72,1024]{1,0:T(8,128)(2,1)S(1)}, f16[72,1024]{1,0:T(8,128)(2,1)S(1)}, u32[]{:S(2)}, u32[]{:S(2)}) collective-permute-start(f16[72,1024]{1,0:T(8,128)(2,1)S(1)} %pad_maximum_fusion.17), channel_id=1, source_target_pairs={{0,128},{1,129},{2,130},{3,131},{4,132},{5,133},{6,134},{7,135},{8... | collective-permute-start | bytes 442376 | tf_op jit(solution)/shard_map/ppermute | solution.py:46
  50.0 2.7 %collective-permute-start.19 = (f16[72,1024]{1,0:T(8,128)(2,1)S(1)}, f16[72,1024]{1,0:T(8,128)(2,1)S(1)}, u32[]{:S(2)}, u32[]{:S(2)}) collective-permute-start(f16[72,1024]{1,0:T(8,128)(2,1)S(1)} %get-tuple-element.81), channel_id=1, source_target_pairs={{0,96},{1,97},{2,98},{3,99},{4,100},{5,101},{6,102},{7,103},{8,104... | collective-permute-start | bytes 442376 | tf_op jit(solution)/shard_map/ppermute | solution.py:46
  53.4 2.8 %collective-permute-start.14 = (bf16[64,1024]{1,0:T(8,128)(2,1)S(1)}, bf16[64,1024]{1,0:T(8,128)(2,1)S(1)}, u32[]{:S(2)}, u32[]{:S(2)}) collective-permute-start(bf16[64,1024]{1,0:T(8,128)(2,1)S(1)} %add_convert_fusion.1), channel_id=1, source_target_pairs={{0,96},{1,97},{2,98},{3,99},{4,100},{5,101},{6,102},{7,103},{8,104... | collective-permute-start | bytes 393224 | tf_op jit(solution)/shard_map/ppermute | solution.py:46
  61.7 4.1 %collective-permute-done.12 = bf16[64,1024]{1,0:T(8,128)(2,1)S(1)} collective-permute-done((bf16[64,1024]{1,0:T(8,128)(2,1)S(1)}, bf16[64,1024]{1,0:T(8,128)(2,1)S(1)}, u32[]{:S(2)}, u32[]{:S(2)}) %collective-permute-start.12) | collective-permute-done | bytes 131104 | tf_op jit(solution)/shard_map/ppermute | solution.py:46
  66.0 2.6 %scores.2 = (f32[8,4,8,1536]{3,2,1,0:T(8,128)S(1)}, f32[8,1536]{1,0:T(8,128)S(1)}) custom-call(bf16[4,64,1024]{2,1,0:T(8,128)(2,1)S(1)} %pad_maximum_fusion.5.low, bf16[768,1024]{1,0:T(8,128)(2,1)S(1)} %copy-done.1, bf16[768,1024]{1,0:T(8,128)(2,1)S(1)} %collective-permute-done.15.far), custom_call_target="tpu_custom_call" | custom-call | flops 805306368 | bytes 4194304 | tf_op jit(solution)/shard_map/scores/pallas_call | solution.py:144
  72.9 2.9 %collective-permute-done.23 = bf16[64,1024]{1,0:T(8,128)(2,1)S(1)} collective-permute-done((bf16[64,1024]{1,0:T(8,128)(2,1)S(1)}, bf16[64,1024]{1,0:T(8,128)(2,1)S(1)}, u32[]{:S(2)}, u32[]{:S(2)}) %collective-permute-start.23) | collective-permute-done | bytes 131104 | tf_op jit(solution)/shard_map/ppermute | solution.py:46
  76.5 2.6 %scores.3 = (f32[8,4,8,1536]{3,2,1,0:T(8,128)S(1)}, f32[8,1536]{1,0:T(8,128)S(1)}) custom-call(bf16[4,64,1024]{2,1,0:T(8,128)(2,1)S(1)} %pad_maximum_fusion.6.low, bf16[768,1024]{1,0:T(8,128)(2,1)S(1)} %copy-done.1, bf16[768,1024]{1,0:T(8,128)(2,1)S(1)} %collective-permute-done.15.far), custom_call_target="tpu_custom_call" | custom-call | flops 805306368 | bytes 4194304 | tf_op jit(solution)/shard_map/scores/pallas_call | solution.py:144
  79.7 7.3 %collective-permute-start.25 = (f16[136,1536]{1,0:T(8,128)(2,1)S(1)}, f16[136,1536]{1,0:T(8,128)(2,1)S(1)}, u32[]{:S(2)}, u32[]{:S(2)}) collective-permute-start(f16[136,1536]{1,0:T(8,128)(2,1)S(1)} %get-tuple-element.78), channel_id=1, source_target_pairs={{0,12},{1,13},{2,14},{3,15},{4,8},{5,9},{6,10},{7,11},{8,4},{9,5},... | collective-permute-start | bytes 1253384 | tf_op jit(solution)/shard_map/ppermute | solution.py:46
  87.0 5.5 %collective-permute-done.25 = f16[136,1536]{1,0:T(8,128)(2,1)S(1)} collective-permute-done((f16[136,1536]{1,0:T(8,128)(2,1)S(1)}, f16[136,1536]{1,0:T(8,128)(2,1)S(1)}, u32[]{:S(2)}, u32[]{:S(2)}) %collective-permute-start.25) | collective-permute-done | bytes 417824 | tf_op jit(solution)/shard_map/ppermute | solution.py:46
  92.6 12.2 %collective-permute-done.24 = f16[136,1536]{1,0:T(8,128)(2,1)S(1)} collective-permute-done((f16[136,1536]{1,0:T(8,128)(2,1)S(1)}, f16[136,1536]{1,0:T(8,128)(2,1)S(1)}, u32[]{:S(2)}, u32[]{:S(2)}) %collective-permute-start.24) | collective-permute-done | bytes 417824 | tf_op jit(solution)/shard_map/ppermute | solution.py:46
  105.3 2.6 %collective-permute-start.28 = (f16[40,1536]{1,0:T(8,128)(2,1)S(1)}, f16[40,1536]{1,0:T(8,128)(2,1)S(1)}, u32[]{:S(2)}, u32[]{:S(2)}) collective-permute-start(f16[40,1536]{1,0:T(8,128)(2,1)S(1)} %get-tuple-element.76), channel_id=1, source_target_pairs={{0,3},{1,2},{2,1},{3,0},{4,7},{5,6},{6,5},{7,4},{8,11},{9,10},{10,... | collective-permute-start | bytes 368648 | tf_op jit(solution)/shard_map/ppermute | solution.py:46
  108.7 2.4 %collective-permute-done.28 = f16[40,1536]{1,0:T(8,128)(2,1)S(1)} collective-permute-done((f16[40,1536]{1,0:T(8,128)(2,1)S(1)}, f16[40,1536]{1,0:T(8,128)(2,1)S(1)}, u32[]{:S(2)}, u32[]{:S(2)}) %collective-permute-start.28) | collective-permute-done | bytes 122912 | tf_op jit(solution)/shard_map/ppermute | solution.py:46
  111.1 2.2 %collective-permute-done.27 = f16[40,1536]{1,0:T(8,128)(2,1)S(1)} collective-permute-done((f16[40,1536]{1,0:T(8,128)(2,1)S(1)}, f16[40,1536]{1,0:T(8,128)(2,1)S(1)}, u32[]{:S(2)}, u32[]{:S(2)}) %collective-permute-start.27) | collective-permute-done | bytes 122912 | tf_op jit(solution)/shard_map/ppermute | solution.py:46
  113.5 2.4 %collective-permute-start.29 = (f32[32,768]{1,0:T(8,128)S(1)}, f32[32,768]{1,0:T(8,128)S(1)}, u32[]{:S(2)}, u32[]{:S(2)}) collective-permute-start(f32[32,768]{1,0:T(8,128)S(1)} %get-tuple-element.62), channel_id=1, source_target_pairs={{0,16},{1,17},{2,18},{3,19},{4,20},{5,21},{6,22},{7,23},{8,24},{9,... | collective-permute-start | bytes 294920 | tf_op jit(solution)/shard_map/ppermute | solution.py:46
  (101 shorter events, 25.0 us)
Async XLA Ops:
  5.1 16.4 %collective-permute-start.6 = (f32[1024,1024]{1,0:T(8,128)}, f32[1024,1024]{1,0:T(8,128)S(1)}, u32[]{:S(2)}, u32[]{:S(2)}) collective-permute-start(f32[1024,1024]{1,0:T(8,128)} %near.1), channel_id=1, source_target_pairs={{0,16},{1,17},{2,18},{3,19},{4,20},{5,21},{6,22},{7,23},{8,24},{9,... | collective-permute-start | bytes 12582920 | tf_op jit(solution)/shard_map/ppermute | solution.py:46
  5.5 6.6 %collective-permute-start.3 = (bf16[32,2048]{1,0:T(8,128)(2,1)S(1)}, bf16[32,2048]{1,0:T(8,128)(2,1)S(1)}, u32[]{:S(2)}, u32[]{:S(2)}) collective-permute-start(bf16[32,2048]{1,0:T(8,128)(2,1)S(1)} %get-tuple-element.71), channel_id=1, source_target_pairs={{0,3},{1,2},{2,1},{3,0},{4,7},{5,6},{6,5},{7,4},{8,11},{9,10},{10,... | collective-permute-start | bytes 393224 | tf_op jit(solution)/shard_map/ppermute | solution.py:46
  6.3 5.8 %collective-permute-start.2 = (bf16[32,2048]{1,0:T(8,128)(2,1)S(1)}, bf16[32,2048]{1,0:T(8,128)(2,1)S(1)}, u32[]{:S(2)}, u32[]{:S(2)}) collective-permute-start(bf16[32,2048]{1,0:T(8,128)(2,1)S(1)} %get-tuple-element.71), channel_id=1, source_target_pairs={{0,2},{1,3},{2,0},{3,1},{4,6},{5,7},{6,4},{7,5},{8,10},{9,11},{10,... | collective-permute-start | bytes 393224 | tf_op jit(solution)/shard_map/ppermute | solution.py:46
  6.8 6.0 %collective-permute-start.1 = (bf16[32,2048]{1,0:T(8,128)(2,1)S(1)}, bf16[32,2048]{1,0:T(8,128)(2,1)S(1)}, u32[]{:S(2)}, u32[]{:S(2)}) collective-permute-start(bf16[32,2048]{1,0:T(8,128)(2,1)S(1)} %get-tuple-element.71), channel_id=1, source_target_pairs={{0,1},{1,0},{2,3},{3,2},{4,5},{5,4},{6,7},{7,6},{8,9},{9,8},{10,11... | collective-permute-start | bytes 393224 | tf_op jit(solution)/shard_map/ppermute | solution.py:46
  13.0 8.4 %collective-permute-start.5 = (bf16[128,2048]{1,0:T(8,128)(2,1)S(1)}, bf16[128,2048]{1,0:T(8,128)(2,1)S(1)}, u32[]{:S(2)}, u32[]{:S(2)}) collective-permute-start(bf16[128,2048]{1,0:T(8,128)(2,1)S(1)} %bitcast.84), channel_id=1, source_target_pairs={{0,4},{1,5},{2,6},{3,7},{4,0},{5,1},{6,2},{7,3},{8,12},{9,13},{10,... | collective-permute-start | bytes 1572872 | tf_op jit(solution)/shard_map/ppermute | solution.py:46
  13.4 15.0 %collective-permute-start.4 = (bf16[128,2048]{1,0:T(8,128)(2,1)S(1)}, bf16[128,2048]{1,0:T(8,128)(2,1)S(1)}, u32[]{:S(2)}, u32[]{:S(2)}) collective-permute-start(bf16[128,2048]{1,0:T(8,128)(2,1)S(1)} %bitcast.85), channel_id=1, source_target_pairs={{0,12},{1,13},{2,14},{3,15},{4,8},{5,9},{6,10},{7,11},{8,4},{9,5},... | collective-permute-start | bytes 1572872 | tf_op jit(solution)/shard_map/ppermute | solution.py:46
  28.7 8.1 %collective-permute-start.9 = (f16[72,1024]{1,0:T(8,128)(2,1)S(1)}, f16[72,1024]{1,0:T(8,128)(2,1)S(1)}, u32[]{:S(2)}, u32[]{:S(2)}) collective-permute-start(f16[72,1024]{1,0:T(8,128)(2,1)S(1)} %get-tuple-element.84), channel_id=1, source_target_pairs={{0,96},{1,97},{2,98},{3,99},{4,100},{5,101},{6,102},{7,103},{8,104... | collective-permute-start | bytes 442376 | tf_op jit(solution)/shard_map/ppermute | solution.py:46
  31.5 5.6 %collective-permute-start.8 = (f16[72,1024]{1,0:T(8,128)(2,1)S(1)}, f16[72,1024]{1,0:T(8,128)(2,1)S(1)}, u32[]{:S(2)}, u32[]{:S(2)}) collective-permute-start(f16[72,1024]{1,0:T(8,128)(2,1)S(1)} %get-tuple-element.83), channel_id=1, source_target_pairs={{0,64},{1,65},{2,66},{3,67},{4,68},{5,69},{6,70},{7,71},{8,72},{9,... | collective-permute-start | bytes 442376 | tf_op jit(solution)/shard_map/ppermute | solution.py:46
  32.2 8.3 %collective-permute-start.10 = (bf16[128,2048]{1,0:T(8,128)(2,1)S(1)}, bf16[128,2048]{1,0:T(8,128)(2,1)S(1)}, u32[]{:S(2)}, u32[]{:S(2)}) collective-permute-start(bf16[128,2048]{1,0:T(8,128)(2,1)S(1)} %collective-permute-done.4), channel_id=1, source_target_pairs={{0,4},{1,5},{2,6},{3,7},{4,0},{5,1},{6,2},{7,3},{8,12},{9,13},{10,... | collective-permute-start | bytes 1572872 | tf_op jit(solution)/shard_map/ppermute | solution.py:46
  32.7 33.3 %collective-permute-start.15 = (bf16[768,1024]{1,0:T(8,128)(2,1)S(1)}, bf16[768,1024]{1,0:T(8,128)(2,1)S(1)}, u32[]{:S(2)}, u32[]{:S(2)}) collective-permute-start(bf16[768,1024]{1,0:T(8,128)(2,1)S(1)} %copy-done.1), channel_id=1, source_target_pairs={{0,16},{1,17},{2,18},{3,19},{4,20},{5,21},{6,22},{7,23},{8,24},{9,... | collective-permute-start | bytes 4718600 | tf_op jit(solution)/shard_map/ppermute | solution.py:46
  44.7 8.6 %collective-permute-start.11 = (f16[72,1024]{1,0:T(8,128)(2,1)S(1)}, f16[72,1024]{1,0:T(8,128)(2,1)S(1)}, u32[]{:S(2)}, u32[]{:S(2)}) collective-permute-start(f16[72,1024]{1,0:T(8,128)(2,1)S(1)} %pad_maximum_fusion.17), channel_id=1, source_target_pairs={{0,128},{1,129},{2,130},{3,131},{4,132},{5,133},{6,134},{7,135},{8... | collective-permute-start | bytes 442376 | tf_op jit(solution)/shard_map/ppermute | solution.py:46
  50.0 6.3 %collective-permute-start.19 = (f16[72,1024]{1,0:T(8,128)(2,1)S(1)}, f16[72,1024]{1,0:T(8,128)(2,1)S(1)}, u32[]{:S(2)}, u32[]{:S(2)}) collective-permute-start(f16[72,1024]{1,0:T(8,128)(2,1)S(1)} %get-tuple-element.81), channel_id=1, source_target_pairs={{0,96},{1,97},{2,98},{3,99},{4,100},{5,101},{6,102},{7,103},{8,104... | collective-permute-start | bytes 442376 | tf_op jit(solution)/shard_map/ppermute | solution.py:46
  52.6 5.6 %collective-permute-start.18 = (f16[72,1024]{1,0:T(8,128)(2,1)S(1)}, f16[72,1024]{1,0:T(8,128)(2,1)S(1)}, u32[]{:S(2)}, u32[]{:S(2)}) collective-permute-start(f16[72,1024]{1,0:T(8,128)(2,1)S(1)} %get-tuple-element.80), channel_id=1, source_target_pairs={{0,64},{1,65},{2,66},{3,67},{4,68},{5,69},{6,70},{7,71},{8,72},{9,... | collective-permute-start | bytes 442376 | tf_op jit(solution)/shard_map/ppermute | solution.py:46
  53.0 7.3 %collective-permute-start.17 = (f16[72,1024]{1,0:T(8,128)(2,1)S(1)}, f16[72,1024]{1,0:T(8,128)(2,1)S(1)}, u32[]{:S(2)}, u32[]{:S(2)}) collective-permute-start(f16[72,1024]{1,0:T(8,128)(2,1)S(1)} %get-tuple-element.79), channel_id=1, source_target_pairs={{0,32},{1,33},{2,34},{3,35},{4,36},{5,37},{6,38},{7,39},{8,40},{9,... | collective-permute-start | bytes 442376 | tf_op jit(solution)/shard_map/ppermute | solution.py:46
  53.4 8.3 %collective-permute-start.14 = (bf16[64,1024]{1,0:T(8,128)(2,1)S(1)}, bf16[64,1024]{1,0:T(8,128)(2,1)S(1)}, u32[]{:S(2)}, u32[]{:S(2)}) collective-permute-start(bf16[64,1024]{1,0:T(8,128)(2,1)S(1)} %add_convert_fusion.1), channel_id=1, source_target_pairs={{0,96},{1,97},{2,98},{3,99},{4,100},{5,101},{6,102},{7,103},{8,104... | collective-permute-start | bytes 393224 | tf_op jit(solution)/shard_map/ppermute | solution.py:46
  58.2 7.6 %collective-permute-start.12 = (bf16[64,1024]{1,0:T(8,128)(2,1)S(1)}, bf16[64,1024]{1,0:T(8,128)(2,1)S(1)}, u32[]{:S(2)}, u32[]{:S(2)}) collective-permute-start(bf16[64,1024]{1,0:T(8,128)(2,1)S(1)} %add_convert_fusion.1), channel_id=1, source_target_pairs={{0,32},{1,33},{2,34},{3,35},{4,36},{5,37},{6,38},{7,39},{8,40},{9,... | collective-permute-start | bytes 393224 | tf_op jit(solution)/shard_map/ppermute | solution.py:46
  60.5 8.3 %collective-permute-start.20 = (f16[72,1024]{1,0:T(8,128)(2,1)S(1)}, f16[72,1024]{1,0:T(8,128)(2,1)S(1)}, u32[]{:S(2)}, u32[]{:S(2)}) collective-permute-start(f16[72,1024]{1,0:T(8,128)(2,1)S(1)} %pad_maximum_fusion.18), channel_id=1, source_target_pairs={{0,128},{1,129},{2,130},{3,131},{4,132},{5,133},{6,134},{7,135},{8... | collective-permute-start | bytes 442376 | tf_op jit(solution)/shard_map/ppermute | solution.py:46
  69.0 6.8 %collective-permute-start.23 = (bf16[64,1024]{1,0:T(8,128)(2,1)S(1)}, bf16[64,1024]{1,0:T(8,128)(2,1)S(1)}, u32[]{:S(2)}, u32[]{:S(2)}) collective-permute-start(bf16[64,1024]{1,0:T(8,128)(2,1)S(1)} %add_convert_fusion), channel_id=1, source_target_pairs={{0,96},{1,97},{2,98},{3,99},{4,100},{5,101},{6,102},{7,103},{8,104... | collective-permute-start | bytes 393224 | tf_op jit(solution)/shard_map/ppermute | solution.py:46
  69.7 6.1 %collective-permute-start.22 = (bf16[64,1024]{1,0:T(8,128)(2,1)S(1)}, bf16[64,1024]{1,0:T(8,128)(2,1)S(1)}, u32[]{:S(2)}, u32[]{:S(2)}) collective-permute-start(bf16[64,1024]{1,0:T(8,128)(2,1)S(1)} %add_convert_fusion), channel_id=1, source_target_pairs={{0,64},{1,65},{2,66},{3,67},{4,68},{5,69},{6,70},{7,71},{8,72},{9,... | collective-permute-start | bytes 393224 | tf_op jit(solution)/shard_map/ppermute | solution.py:46
  70.8 5.6 %collective-permute-start.21 = (bf16[64,1024]{1,0:T(8,128)(2,1)S(1)}, bf16[64,1024]{1,0:T(8,128)(2,1)S(1)}, u32[]{:S(2)}, u32[]{:S(2)}) collective-permute-start(bf16[64,1024]{1,0:T(8,128)(2,1)S(1)} %add_convert_fusion), channel_id=1, source_target_pairs={{0,32},{1,33},{2,34},{3,35},{4,36},{5,37},{6,38},{7,39},{8,40},{9,... | collective-permute-start | bytes 393224 | tf_op jit(solution)/shard_map/ppermute | solution.py:46
  72.5 14.6 %collective-permute-start.16 = (f16[136,1536]{1,0:T(8,128)(2,1)S(1)}, f16[136,1536]{1,0:T(8,128)(2,1)S(1)}, u32[]{:S(2)}, u32[]{:S(2)}) collective-permute-start(f16[136,1536]{1,0:T(8,128)(2,1)S(1)} %pad_maximum_fusion.7), channel_id=1, source_target_pairs={{0,4},{1,5},{2,6},{3,7},{4,0},{5,1},{6,2},{7,3},{8,12},{9,13},{10,... | collective-permute-start | bytes 1253384 | tf_op jit(solution)/shard_map/ppermute | solution.py:46
  79.7 12.9 %collective-permute-start.25 = (f16[136,1536]{1,0:T(8,128)(2,1)S(1)}, f16[136,1536]{1,0:T(8,128)(2,1)S(1)}, u32[]{:S(2)}, u32[]{:S(2)}) collective-permute-start(f16[136,1536]{1,0:T(8,128)(2,1)S(1)} %get-tuple-element.78), channel_id=1, source_target_pairs={{0,12},{1,13},{2,14},{3,15},{4,8},{5,9},{6,10},{7,11},{8,4},{9,5},... | collective-permute-start | bytes 1253384 | tf_op jit(solution)/shard_map/ppermute | solution.py:46
  87.0 17.7 %collective-permute-start.24 = (f16[136,1536]{1,0:T(8,128)(2,1)S(1)}, f16[136,1536]{1,0:T(8,128)(2,1)S(1)}, u32[]{:S(2)}, u32[]{:S(2)}) collective-permute-start(f16[136,1536]{1,0:T(8,128)(2,1)S(1)} %get-tuple-element.77), channel_id=1, source_target_pairs={{0,8},{1,9},{2,10},{3,11},{4,12},{5,13},{6,14},{7,15},{8,0},{9,1},... | collective-permute-start | bytes 1253384 | tf_op jit(solution)/shard_map/ppermute | solution.py:46
  105.3 5.7 %collective-permute-start.28 = (f16[40,1536]{1,0:T(8,128)(2,1)S(1)}, f16[40,1536]{1,0:T(8,128)(2,1)S(1)}, u32[]{:S(2)}, u32[]{:S(2)}) collective-permute-start(f16[40,1536]{1,0:T(8,128)(2,1)S(1)} %get-tuple-element.76), channel_id=1, source_target_pairs={{0,3},{1,2},{2,1},{3,0},{4,7},{5,6},{6,5},{7,4},{8,11},{9,10},{10,... | collective-permute-start | bytes 368648 | tf_op jit(solution)/shard_map/ppermute | solution.py:46
  (8 other events, 40.0 us)

commit v3 on v2

--- a/solution.py
+++ b/solution.py
@@ -74,88 +74,104 @@
     return (lax.axis_index("row") // CORE) % Y
 
 
-def note_top(i, acc, most, top):
-    @pl.when(i == 0)
-    def _():
-        most[...] = jnp.zeros(most.shape, F32)
-
-    most[...] = jnp.maximum(most[...], jnp.max(jnp.abs(acc).reshape(-1, 8, acc.shape[1]), axis=0))
-
-    @pl.when(i == pl.num_programs(0) - 1)
-    def _():
-        bound = jnp.broadcast_to(jnp.max(most[...]), top.shape)
-        top[...] = jnp.clip(15.0 - jnp.ceil(jnp.log2(bound)), -100.0, 100.0)
-
-
-def precond_kernel(tests, near, far, out, top, most):
-    i, y = pl.program_id(0), y_place()
-    rows, width = tests.shape[0], near.shape[0]
-    acc = None
-    for at, gram in ((0, near), (width, far)):
-        high = gram[...].astype(BF16)
-        low = (gram[...] - high.astype(F32)).astype(BF16)
-        for part in (high, low):
-            new = jnp.dot(tests[:, at : at + width], part, preferred_element_type=F32)
-            acc = new if acc is None else acc + new
-    parts = acc.reshape(out.shape[1], Y, out.shape[2], -1)
-    for quarter in range(Y):
-        out[quarter ^ y] = parts[:, quarter]
-    note_top(i, acc, most, top)
-
-
-def scores_kernel(low, near, far, out, top, most):
-    i, y = pl.program_id(0), y_place()
+def exponent_of(most, top):
+    bound = jnp.broadcast_to(jnp.max(most), top.shape)
+    top[...] = jnp.clip(15.0 - jnp.ceil(jnp.log2(bound)), -100.0, 100.0)
+
+
+def largest(most, acc):
+    new = jnp.max(jnp.abs(acc).reshape(-1, 8, acc.shape[1]), axis=0)
+    return new if most is None else jnp.maximum(most, new)
+
+
+def precond_kernel(tests, near, far, out, top):
+    y, width, step = y_place(), near.shape[0], 512
+    most = None
+    for i in range(0, near.shape[1], step):
+        acc = None
+        for at, gram in ((0, near), (width, far)):
+            gram = gram[:, i : i + step]
+            high = gram.astype(BF16)
+            low = (gram - high.astype(F32)).astype(BF16)
+            for part in (high, low):
+                new = jnp.dot(tests[:, at : at + width], part, preferred_element_type=F32)
+                acc = new if acc is None else acc + new
+        parts = acc.reshape(out.shape[1], Y, out.shape[2], step)
+        for quarter in range(Y):
+            out[quarter ^ y, :, :, i : i + step] = parts[:, quarter]
+        most = largest(most, acc)
+    exponent_of(most, top)
+
+
+def scores_kernel(low, near, far, out, top):
+    y, trains = y_place(), near.shape[0]
     tests = low[...].reshape(-1, low.shape[2])
-
-    def product(trains):
+    most = None
+    for at, block in ((0, near), (trains, far)):
         acc = lax.dot_general(
-            tests, trains[...], (((1,), (1,)), ((), ())), preferred_element_type=F32
+            tests, block[...], (((1,), (1,)), ((), ())), preferred_element_type=F32
         )
-        parts = acc.reshape(Y, out.shape[0], out.shape[2], -1)
+        parts = acc.reshape(Y, out.shape[0], out.shape[2], trains)
         for k in range(Y):
-            out[:, k ^ y] = parts[k]
-        note_top(i, acc, most, top)
-
-    pl.when(i < pl.num_programs(0) // 2)(lambda: product(near))
-    pl.when(i >= pl.num_programs(0) // 2)(lambda: product(far))
+            out[:, k ^ y, :, at : at + trains] = parts[k]
+        most = largest(most, acc)
+    exponent_of(most, top)
 
 
 def precond(tests, near, far):
     rows, (width, depth) = tests.shape[0], near.shape
-    slots, group, step = rows // 32, 8, 256
-    block = pl.BlockSpec((width, step), lambda i: (0, i))
     return pl.pallas_call(
         precond_kernel,
-        grid=(depth // step,),
-        in_specs=[VMEM, block, block],
-        out_specs=(pl.BlockSpec((Y, slots, group, step), lambda i: (0, 0, 0, i)), pl.BlockSpec((8, depth), lambda i: (0, 0))),
-        out_shape=(jax.ShapeDtypeStruct((Y, slots, group, depth), F32), jax.ShapeDtypeStruct((8, depth), F32)),
-        scratch_shapes=[pltpu.VMEM((8, step), F32)],
+        in_specs=[VMEM] * 3,
+        out_specs=(VMEM, VMEM),
+        out_shape=(
+            jax.ShapeDtypeStruct((Y, rows // 32, 8, depth), F32),
+            jax.ShapeDtypeStruct((8, depth), F32),
+        ),
         compiler_params=PARAMS,
-        cost_estimate=pl.CostEstimate(flops=8 * rows * width * depth, bytes_accessed=2**23, transcendentals=0),
+        cost_estimate=pl.CostEstimate(
+            flops=8 * rows * width * depth, bytes_accessed=2**23, transcendentals=0
+        ),
         name="precond",
     )(tests, near, far)
 
 
 def scores_of(low, near, far):
     trains, depth = near.shape
-    slots, group, step = low.shape[1] // 8, 8, 256
-    n = trains // step
     return pl.pallas_call(
         scores_kernel,
-        grid=(2 * n,),
-        in_specs=[
-            VMEM,
-            pl.BlockSpec((step, depth), lambda i: (jnp.minimum(i, n - 1), 0)),
-            pl.BlockSpec((step, depth), lambda i: (jnp.maximum(i - n, 0), 0)),
-        ],
-        out_specs=(pl.BlockSpec((slots, Y, group, step), lambda i: (0, 0, 0, i)), pl.BlockSpec((8, 2 * trains), lambda i: (0, 0))),
-        out_shape=(jax.ShapeDtypeStruct((slots, Y, group, 2 * trains), F32), jax.ShapeDtypeStruct((8, 2 * trains), F32)),
-        scratch_shapes=[pltpu.VMEM((8, step), F32)],
+        in_specs=[VMEM] * 3,
+        out_specs=(VMEM, VMEM),
+        out_shape=(
+            jax.ShapeDtypeStruct((low.shape[1] // 8, Y, 8, 2 * trains), F32),
+            jax.ShapeDtypeStruct((8, 2 * trains), F32),
+        ),
         compiler_params=PARAMS,
-        cost_estimate=pl.CostEstimate(flops=4 * low.shape[0] * low.shape[1] * trains * depth, bytes_accessed=2**22, transcendentals=0),
+        cost_estimate=pl.CostEstimate(
+            flops=4 * low.shape[0] * low.shape[1] * trains * depth,
+            bytes_accessed=2**22,
+            transcendentals=0,
+        ),
         name="scores",
     )(low, near, far)
+
+
+def near_kernel(gram, out, sem):
+    copy = pltpu.make_async_copy(gram, out, sem)
+    copy.start()
+    copy.wait()
+
+
+def brought_in(gram):
+    return pl.pallas_call(
+        near_kernel,
+        in_specs=[pl.BlockSpec(memory_space=pl.ANY)],
+        out_specs=VMEM,
+        out_shape=jax.ShapeDtypeStruct(gram.shape, F32),
+        scratch_shapes=[pltpu.SemaphoreType.DMA],
+        compiler_params=PARAMS,
+        name="brought_in",
+    )(gram)
 
 
 def per_device(test_grads, inverse_gram, train_grads):
@@ -173,8 +189,10 @@
 
     block = jnp.concatenate([mine, got], axis=1)
     block = gather(block, FIRST).reshape(4 * half, 2 * width)
+    near = brought_in(inverse_gram)
+    block, near = lax.optimization_barrier((block, near))
     slot1, slot3 = send(block, SECOND[1]), send(block, SECOND[3])
-    part = precond(jnp.concatenate([block, slot1]), inverse_gram, far_gram)
+    part = precond(jnp.concatenate([block, slot1]), near, far_gram)
     slot3, part = lax.optimization_barrier((slot3, part))
     slot2 = send(slot3, SECOND[1])
 
@@ -191,7 +209,7 @@
         return [(scores[j], e[:1]) for j in range(2)]
 
     first = summed(*part)
-    part = precond(jnp.concatenate([slot2, slot3]), inverse_gram, far_gram)
+    part = precond(jnp.concatenate([slot2, slot3]), near, far_gram)
     first, part = lax.optimization_barrier((first, part))
     second = summed(*part)
     low0 = rounded(*first)

time: 118 us -> 114 us (0.966); the launches traced: 118 us -> 112 us
  starting transfers between devices: 50.1 us -> 43.5 us
  waiting for transfers between devices: 47 us -> 53.5 us
  Pallas kernels: 13 us -> 7.83 us
    ppermute x30, starting transfers between devices: 50.1 us -> 43.5 us  [send(): return lax.ppermute(value, BOTH, perm)]
    ppermute x30, waiting for transfers between devices: 47 us -> 53.5 us  [send(): return lax.ppermute(value, BOTH, perm)]
    pallas_call x4 -> x5, Pallas kernels: 13 us -> 7.83 us  [the longest x2 5.19 us: precond(): pl.pallas_call(precond_kernel, in_specs=[VMEM] * 3, out_specs=(VMEM, VMEM...]
  transfers between devices with their start and end apart: 30 -> 30, of which waited for: 18 -> 21; matrix products, arithmetic and copies ran while one was open for 2% -> 2% of each run, Pallas kernels for 11% -> 7%
where the time goes in v3:
time: 114 us; the launch traced here: 112 us
  waiting for transfers between devices  53.5 us (47%)
  starting transfers between devices  43.5 us (38%)
  Pallas kernels  7.83 us (7%)
  other arithmetic  4.44 us (4%)
  local copies, waits for them, and re-layouts  2.54 us (2%)
    ppermute x30, waiting for transfers between devices, send(): return lax.ppermute(value, BOTH, perm)  53.5 us
    ppermute x30, starting transfers between devices, send(): return lax.ppermute(value, BOTH, perm)  43.5 us
    pallas_call x2, Pallas kernels, precond(): pl.pallas_call(precond_kernel, in_specs=[VMEM] * 3, out_specs=(VMEM, VMEM...  5.19 us
    pallas_call x2, Pallas kernels, scores_of(): pl.pallas_call(scores_kernel, in_specs=[VMEM] * 3, out_specs=(VMEM, VMEM)...  2.35 us
  transfers between devices with their start and end apart: 30, of which 21 were waited for; matrix products, arithmetic and copies ran while one was open for 2% of the time, Pallas kernels for 7%

profile of v3, /device:TPU:1, one launch (start us, length us, event | category | flops | bytes accessed | tf_op | source)
XLA Modules:
  0.0 112.2 jit_solution(9736179922145703020)
XLA Ops:
  0.9 3.3 %collective-permute-start = (bf16[32,1024]{1,0:T(8,128)(2,1)S(1)}, bf16[32,1024]{1,0:T(8,128)(2,1)S(1)}, u32[]{:S(2)}, u32[]{:S(2)}) collective-permute-start(bf16[32,1024]{1,0:T(8,128)(2,1)S(1)} %get-tuple-element.77), channel_id=1, source_target_pairs={{0,16},{1,17},{2,18},{3,19},{4,20},{5,21},{6,22},{7,23},{8,24},{9,... | collective-permute-start | bytes 196616 | tf_op jit(solution)/shard_map/ppermute | solution.py:46
  6.8 2.0 %collective-permute-start.1 = (bf16[32,2048]{1,0:T(8,128)(2,1)S(1)}, bf16[32,2048]{1,0:T(8,128)(2,1)S(1)}, u32[]{:S(2)}, u32[]{:S(2)}) collective-permute-start(bf16[32,2048]{1,0:T(8,128)(2,1)S(1)} %get-tuple-element.75), channel_id=1, source_target_pairs={{0,1},{1,0},{2,3},{3,2},{4,5},{5,4},{6,7},{7,6},{8,9},{9,8},{10,11... | collective-permute-start | bytes 393224 | tf_op jit(solution)/shard_map/ppermute | solution.py:46
  8.8 2.2 %copy-done.1 = f32[1024,1024]{1,0:T(8,128)S(1)} copy-done((f32[1024,1024]{1,0:T(8,128)S(1)}, f32[1024,1024]{1,0:T(8,128)}, u32[]{:S(2)}) %copy-start.1) | copy-done | bytes 4194328
  13.4 2.8 %collective-permute-start.4 = (bf16[128,2048]{1,0:T(8,128)(2,1)S(1)}, bf16[128,2048]{1,0:T(8,128)(2,1)S(1)}, u32[]{:S(2)}, u32[]{:S(2)}) collective-permute-start(bf16[128,2048]{1,0:T(8,128)(2,1)S(1)} %bitcast.85), channel_id=1, source_target_pairs={{0,12},{1,13},{2,14},{3,15},{4,8},{5,9},{6,10},{7,11},{8,4},{9,5},... | collective-permute-start | bytes 1572872 | tf_op jit(solution)/shard_map/ppermute | solution.py:46
  16.3 5.1 %collective-permute-done.5 = bf16[128,2048]{1,0:T(8,128)(2,1)S(1)} collective-permute-done((bf16[128,2048]{1,0:T(8,128)(2,1)S(1)}, bf16[128,2048]{1,0:T(8,128)(2,1)S(1)}, u32[]{:S(2)}, u32[]{:S(2)}) %collective-permute-start.5) | collective-permute-done | bytes 524320 | tf_op jit(solution)/shard_map/ppermute | solution.py:46
  21.5 2.6 %precond.2 = (f32[4,8,8,1024]{3,2,1,0:T(8,128)S(1)}, f32[8,1024]{1,0:T(8,128)S(1)}) custom-call(bf16[256,2048]{1,0:T(8,128)(2,1)S(1)} %pad_maximum_fusion.tests, f32[1024,1024]{1,0:T(8,128)S(1)} %brought_in.1.near, f32[1024,1024]{1,0:T(8,128)S(1)} %collective-permute-done.6.far), custom_call_target="tpu_custom_call" | custom-call | flops 2147483648 | bytes 8388608 | tf_op jit(solution)/shard_map/precond/pallas_call | solution.py:123
  24.1 4.3 %collective-permute-done.4 = bf16[128,2048]{1,0:T(8,128)(2,1)S(1)} collective-permute-done((bf16[128,2048]{1,0:T(8,128)(2,1)S(1)}, bf16[128,2048]{1,0:T(8,128)(2,1)S(1)}, u32[]{:S(2)}, u32[]{:S(2)}) %collective-permute-start.4) | collective-permute-done | bytes 524320 | tf_op jit(solution)/shard_map/ppermute | solution.py:46
  28.7 2.8 %collective-permute-start.9 = (f16[72,1024]{1,0:T(8,128)(2,1)S(1)}, f16[72,1024]{1,0:T(8,128)(2,1)S(1)}, u32[]{:S(2)}, u32[]{:S(2)}) collective-permute-start(f16[72,1024]{1,0:T(8,128)(2,1)S(1)} %get-tuple-element.88), channel_id=1, source_target_pairs={{0,96},{1,97},{2,98},{3,99},{4,100},{5,101},{6,102},{7,103},{8,104... | collective-permute-start | bytes 442376 | tf_op jit(solution)/shard_map/ppermute | solution.py:46
  33.2 4.5 %collective-permute-done.9 = f16[72,1024]{1,0:T(8,128)(2,1)S(1)} collective-permute-done((f16[72,1024]{1,0:T(8,128)(2,1)S(1)}, f16[72,1024]{1,0:T(8,128)(2,1)S(1)}, u32[]{:S(2)}, u32[]{:S(2)}) %collective-permute-start.9) | collective-permute-done | bytes 147488 | tf_op jit(solution)/shard_map/ppermute | solution.py:46
  40.6 2.6 %precond.3 = (f32[4,8,8,1024]{3,2,1,0:T(8,128)S(1)}, f32[8,1024]{1,0:T(8,128)S(1)}) custom-call(bf16[256,2048]{1,0:T(8,128)(2,1)S(1)} %pad_maximum_fusion.1.tests, f32[1024,1024]{1,0:T(8,128)S(1)} %brought_in.1.near, f32[1024,1024]{1,0:T(8,128)S(1)} %collective-permute-done.6.far), custom_call_target="tpu_custom_call" | custom-call | flops 2147483648 | bytes 8388608 | tf_op jit(solution)/shard_map/precond/pallas_call | solution.py:123
  43.4 5.2 %collective-permute-start.11 = (f16[72,1024]{1,0:T(8,128)(2,1)S(1)}, f16[72,1024]{1,0:T(8,128)(2,1)S(1)}, u32[]{:S(2)}, u32[]{:S(2)}) collective-permute-start(f16[72,1024]{1,0:T(8,128)(2,1)S(1)} %pad_maximum_fusion.17), channel_id=1, source_target_pairs={{0,128},{1,129},{2,130},{3,131},{4,132},{5,133},{6,134},{7,135},{8... | collective-permute-start | bytes 442376 | tf_op jit(solution)/shard_map/ppermute | solution.py:46
  48.8 2.7 %collective-permute-start.19 = (f16[72,1024]{1,0:T(8,128)(2,1)S(1)}, f16[72,1024]{1,0:T(8,128)(2,1)S(1)}, u32[]{:S(2)}, u32[]{:S(2)}) collective-permute-start(f16[72,1024]{1,0:T(8,128)(2,1)S(1)} %get-tuple-element.85), channel_id=1, source_target_pairs={{0,96},{1,97},{2,98},{3,99},{4,100},{5,101},{6,102},{7,103},{8,104... | collective-permute-start | bytes 442376 | tf_op jit(solution)/shard_map/ppermute | solution.py:46
  52.5 2.6 %collective-permute-start.14 = (bf16[64,1024]{1,0:T(8,128)(2,1)S(1)}, bf16[64,1024]{1,0:T(8,128)(2,1)S(1)}, u32[]{:S(2)}, u32[]{:S(2)}) collective-permute-start(bf16[64,1024]{1,0:T(8,128)(2,1)S(1)} %add_convert_fusion.1), channel_id=1, source_target_pairs={{0,96},{1,97},{2,98},{3,99},{4,100},{5,101},{6,102},{7,103},{8,104... | collective-permute-start | bytes 393224 | tf_op jit(solution)/shard_map/ppermute | solution.py:46
  55.1 2.5 %collective-permute-done.19 = f16[72,1024]{1,0:T(8,128)(2,1)S(1)} collective-permute-done((f16[72,1024]{1,0:T(8,128)(2,1)S(1)}, f16[72,1024]{1,0:T(8,128)(2,1)S(1)}, u32[]{:S(2)}, u32[]{:S(2)}) %collective-permute-start.19) | collective-permute-done | bytes 147488 | tf_op jit(solution)/shard_map/ppermute | solution.py:46
  57.6 4.1 %collective-permute-start.12 = (bf16[64,1024]{1,0:T(8,128)(2,1)S(1)}, bf16[64,1024]{1,0:T(8,128)(2,1)S(1)}, u32[]{:S(2)}, u32[]{:S(2)}) collective-permute-start(bf16[64,1024]{1,0:T(8,128)(2,1)S(1)} %add_convert_fusion.1), channel_id=1, source_target_pairs={{0,32},{1,33},{2,34},{3,35},{4,36},{5,37},{6,38},{7,39},{8,40},{9,... | collective-permute-start | bytes 393224 | tf_op jit(solution)/shard_map/ppermute | solution.py:46
  63.2 3.2 %collective-permute-done.12 = bf16[64,1024]{1,0:T(8,128)(2,1)S(1)} collective-permute-done((bf16[64,1024]{1,0:T(8,128)(2,1)S(1)}, bf16[64,1024]{1,0:T(8,128)(2,1)S(1)}, u32[]{:S(2)}, u32[]{:S(2)}) %collective-permute-start.12) | collective-permute-done | bytes 131104 | tf_op jit(solution)/shard_map/ppermute | solution.py:46
  68.0 2.2 %collective-permute-done.20 = f16[72,1024]{1,0:T(8,128)(2,1)S(1)} collective-permute-done((f16[72,1024]{1,0:T(8,128)(2,1)S(1)}, f16[72,1024]{1,0:T(8,128)(2,1)S(1)}, u32[]{:S(2)}, u32[]{:S(2)}) %collective-permute-start.20) | collective-permute-done | bytes 147488 | tf_op jit(solution)/shard_map/ppermute | solution.py:46
  74.2 2.5 %collective-permute-done.23 = bf16[64,1024]{1,0:T(8,128)(2,1)S(1)} collective-permute-done((bf16[64,1024]{1,0:T(8,128)(2,1)S(1)}, bf16[64,1024]{1,0:T(8,128)(2,1)S(1)}, u32[]{:S(2)}, u32[]{:S(2)}) %collective-permute-start.23) | collective-permute-done | bytes 131104 | tf_op jit(solution)/shard_map/ppermute | solution.py:46
  79.2 3.0 %collective-permute-start.25 = (f16[136,1536]{1,0:T(8,128)(2,1)S(1)}, f16[136,1536]{1,0:T(8,128)(2,1)S(1)}, u32[]{:S(2)}, u32[]{:S(2)}) collective-permute-start(f16[136,1536]{1,0:T(8,128)(2,1)S(1)} %get-tuple-element.82), channel_id=1, source_target_pairs={{0,12},{1,13},{2,14},{3,15},{4,8},{5,9},{6,10},{7,11},{8,4},{9,5},... | collective-permute-start | bytes 1253384 | tf_op jit(solution)/shard_map/ppermute | solution.py:46
  82.2 2.6 %collective-permute-start.24 = (f16[136,1536]{1,0:T(8,128)(2,1)S(1)}, f16[136,1536]{1,0:T(8,128)(2,1)S(1)}, u32[]{:S(2)}, u32[]{:S(2)}) collective-permute-start(f16[136,1536]{1,0:T(8,128)(2,1)S(1)} %get-tuple-element.81), channel_id=1, source_target_pairs={{0,8},{1,9},{2,10},{3,11},{4,12},{5,13},{6,14},{7,15},{8,0},{9,1},... | collective-permute-start | bytes 1253384 | tf_op jit(solution)/shard_map/ppermute | solution.py:46
  84.8 4.3 %collective-permute-done.25 = f16[136,1536]{1,0:T(8,128)(2,1)S(1)} collective-permute-done((f16[136,1536]{1,0:T(8,128)(2,1)S(1)}, f16[136,1536]{1,0:T(8,128)(2,1)S(1)}, u32[]{:S(2)}, u32[]{:S(2)}) %collective-permute-start.25) | collective-permute-done | bytes 417824 | tf_op jit(solution)/shard_map/ppermute | solution.py:46
  89.1 13.3 %collective-permute-done.24 = f16[136,1536]{1,0:T(8,128)(2,1)S(1)} collective-permute-done((f16[136,1536]{1,0:T(8,128)(2,1)S(1)}, f16[136,1536]{1,0:T(8,128)(2,1)S(1)}, u32[]{:S(2)}, u32[]{:S(2)}) %collective-permute-start.24) | collective-permute-done | bytes 417824 | tf_op jit(solution)/shard_map/ppermute | solution.py:46
  104.6 1.9 %collective-permute-start.26 = (f16[40,1536]{1,0:T(8,128)(2,1)S(1)}, f16[40,1536]{1,0:T(8,128)(2,1)S(1)}, u32[]{:S(2)}, u32[]{:S(2)}) collective-permute-start(f16[40,1536]{1,0:T(8,128)(2,1)S(1)} %get-tuple-element.78), channel_id=1, source_target_pairs={{0,1},{1,0},{2,3},{3,2},{4,5},{5,4},{6,7},{7,6},{8,9},{9,8},{10,11... | collective-permute-start | bytes 368648 | tf_op jit(solution)/shard_map/ppermute | solution.py:46
  106.4 3.0 %collective-permute-done.28 = f16[40,1536]{1,0:T(8,128)(2,1)S(1)} collective-permute-done((f16[40,1536]{1,0:T(8,128)(2,1)S(1)}, f16[40,1536]{1,0:T(8,128)(2,1)S(1)}, u32[]{:S(2)}, u32[]{:S(2)}) %collective-permute-start.28) | collective-permute-done | bytes 122912 | tf_op jit(solution)/shard_map/ppermute | solution.py:46
  (102 shorter events, 26.5 us)
Async XLA Ops:
  5.1 16.4 %collective-permute-start.6 = (f32[1024,1024]{1,0:T(8,128)}, f32[1024,1024]{1,0:T(8,128)S(1)}, u32[]{:S(2)}, u32[]{:S(2)}) collective-permute-start(f32[1024,1024]{1,0:T(8,128)} %gram), channel_id=1, source_target_pairs={{0,16},{1,17},{2,18},{3,19},{4,20},{5,21},{6,22},{7,23},{8,24},{9,... | collective-permute-start | bytes 12582920 | tf_op jit(solution)/shard_map/ppermute | solution.py:46
  5.5 6.6 %collective-permute-start.3 = (bf16[32,2048]{1,0:T(8,128)(2,1)S(1)}, bf16[32,2048]{1,0:T(8,128)(2,1)S(1)}, u32[]{:S(2)}, u32[]{:S(2)}) collective-permute-start(bf16[32,2048]{1,0:T(8,128)(2,1)S(1)} %get-tuple-element.75), channel_id=1, source_target_pairs={{0,3},{1,2},{2,1},{3,0},{4,7},{5,6},{6,5},{7,4},{8,11},{9,10},{10,... | collective-permute-start | bytes 393224 | tf_op jit(solution)/shard_map/ppermute | solution.py:46
  6.3 5.8 %collective-permute-start.2 = (bf16[32,2048]{1,0:T(8,128)(2,1)S(1)}, bf16[32,2048]{1,0:T(8,128)(2,1)S(1)}, u32[]{:S(2)}, u32[]{:S(2)}) collective-permute-start(bf16[32,2048]{1,0:T(8,128)(2,1)S(1)} %get-tuple-element.75), channel_id=1, source_target_pairs={{0,2},{1,3},{2,0},{3,1},{4,6},{5,7},{6,4},{7,5},{8,10},{9,11},{10,... | collective-permute-start | bytes 393224 | tf_op jit(solution)/shard_map/ppermute | solution.py:46
  6.8 6.0 %collective-permute-start.1 = (bf16[32,2048]{1,0:T(8,128)(2,1)S(1)}, bf16[32,2048]{1,0:T(8,128)(2,1)S(1)}, u32[]{:S(2)}, u32[]{:S(2)}) collective-permute-start(bf16[32,2048]{1,0:T(8,128)(2,1)S(1)} %get-tuple-element.75), channel_id=1, source_target_pairs={{0,1},{1,0},{2,3},{3,2},{4,5},{5,4},{6,7},{7,6},{8,9},{9,8},{10,11... | collective-permute-start | bytes 393224 | tf_op jit(solution)/shard_map/ppermute | solution.py:46
  13.0 8.4 %collective-permute-start.5 = (bf16[128,2048]{1,0:T(8,128)(2,1)S(1)}, bf16[128,2048]{1,0:T(8,128)(2,1)S(1)}, u32[]{:S(2)}, u32[]{:S(2)}) collective-permute-start(bf16[128,2048]{1,0:T(8,128)(2,1)S(1)} %bitcast.84), channel_id=1, source_target_pairs={{0,4},{1,5},{2,6},{3,7},{4,0},{5,1},{6,2},{7,3},{8,12},{9,13},{10,... | collective-permute-start | bytes 1572872 | tf_op jit(solution)/shard_map/ppermute | solution.py:46
  13.4 15.0 %collective-permute-start.4 = (bf16[128,2048]{1,0:T(8,128)(2,1)S(1)}, bf16[128,2048]{1,0:T(8,128)(2,1)S(1)}, u32[]{:S(2)}, u32[]{:S(2)}) collective-permute-start(bf16[128,2048]{1,0:T(8,128)(2,1)S(1)} %bitcast.85), channel_id=1, source_target_pairs={{0,12},{1,13},{2,14},{3,15},{4,8},{5,9},{6,10},{7,11},{8,4},{9,5},... | collective-permute-start | bytes 1572872 | tf_op jit(solution)/shard_map/ppermute | solution.py:46
  28.7 9.0 %collective-permute-start.9 = (f16[72,1024]{1,0:T(8,128)(2,1)S(1)}, f16[72,1024]{1,0:T(8,128)(2,1)S(1)}, u32[]{:S(2)}, u32[]{:S(2)}) collective-permute-start(f16[72,1024]{1,0:T(8,128)(2,1)S(1)} %get-tuple-element.88), channel_id=1, source_target_pairs={{0,96},{1,97},{2,98},{3,99},{4,100},{5,101},{6,102},{7,103},{8,104... | collective-permute-start | bytes 442376 | tf_op jit(solution)/shard_map/ppermute | solution.py:46
  31.5 7.0 %collective-permute-start.8 = (f16[72,1024]{1,0:T(8,128)(2,1)S(1)}, f16[72,1024]{1,0:T(8,128)(2,1)S(1)}, u32[]{:S(2)}, u32[]{:S(2)}) collective-permute-start(f16[72,1024]{1,0:T(8,128)(2,1)S(1)} %get-tuple-element.87), channel_id=1, source_target_pairs={{0,64},{1,65},{2,66},{3,67},{4,68},{5,69},{6,70},{7,71},{8,72},{9,... | collective-permute-start | bytes 442376 | tf_op jit(solution)/shard_map/ppermute | solution.py:46
  31.9 7.5 %collective-permute-start.7 = (f16[72,1024]{1,0:T(8,128)(2,1)S(1)}, f16[72,1024]{1,0:T(8,128)(2,1)S(1)}, u32[]{:S(2)}, u32[]{:S(2)}) collective-permute-start(f16[72,1024]{1,0:T(8,128)(2,1)S(1)} %get-tuple-element.86), channel_id=1, source_target_pairs={{0,32},{1,33},{2,34},{3,35},{4,36},{5,37},{6,38},{7,39},{8,40},{9,... | collective-permute-start | bytes 442376 | tf_op jit(solution)/shard_map/ppermute | solution.py:46
  32.2 8.3 %collective-permute-start.10 = (bf16[128,2048]{1,0:T(8,128)(2,1)S(1)}, bf16[128,2048]{1,0:T(8,128)(2,1)S(1)}, u32[]{:S(2)}, u32[]{:S(2)}) collective-permute-start(bf16[128,2048]{1,0:T(8,128)(2,1)S(1)} %collective-permute-done.4), channel_id=1, source_target_pairs={{0,4},{1,5},{2,6},{3,7},{4,0},{5,1},{6,2},{7,3},{8,12},{9,13},{10,... | collective-permute-start | bytes 1572872 | tf_op jit(solution)/shard_map/ppermute | solution.py:46
  32.7 33.8 %collective-permute-start.15 = (bf16[768,1024]{1,0:T(8,128)(2,1)S(1)}, bf16[768,1024]{1,0:T(8,128)(2,1)S(1)}, u32[]{:S(2)}, u32[]{:S(2)}) collective-permute-start(bf16[768,1024]{1,0:T(8,128)(2,1)S(1)} %copy-done), channel_id=1, source_target_pairs={{0,16},{1,17},{2,18},{3,19},{4,20},{5,21},{6,22},{7,23},{8,24},{9,... | collective-permute-start | bytes 4718600 | tf_op jit(solution)/shard_map/ppermute | solution.py:46
  43.4 9.1 %collective-permute-start.11 = (f16[72,1024]{1,0:T(8,128)(2,1)S(1)}, f16[72,1024]{1,0:T(8,128)(2,1)S(1)}, u32[]{:S(2)}, u32[]{:S(2)}) collective-permute-start(f16[72,1024]{1,0:T(8,128)(2,1)S(1)} %pad_maximum_fusion.17), channel_id=1, source_target_pairs={{0,128},{1,129},{2,130},{3,131},{4,132},{5,133},{6,134},{7,135},{8... | collective-permute-start | bytes 442376 | tf_op jit(solution)/shard_map/ppermute | solution.py:46
  48.8 8.8 %collective-permute-start.19 = (f16[72,1024]{1,0:T(8,128)(2,1)S(1)}, f16[72,1024]{1,0:T(8,128)(2,1)S(1)}, u32[]{:S(2)}, u32[]{:S(2)}) collective-permute-start(f16[72,1024]{1,0:T(8,128)(2,1)S(1)} %get-tuple-element.85), channel_id=1, source_target_pairs={{0,96},{1,97},{2,98},{3,99},{4,100},{5,101},{6,102},{7,103},{8,104... | collective-permute-start | bytes 442376 | tf_op jit(solution)/shard_map/ppermute | solution.py:46
  51.5 6.1 %collective-permute-start.18 = (f16[72,1024]{1,0:T(8,128)(2,1)S(1)}, f16[72,1024]{1,0:T(8,128)(2,1)S(1)}, u32[]{:S(2)}, u32[]{:S(2)}) collective-permute-start(f16[72,1024]{1,0:T(8,128)(2,1)S(1)} %get-tuple-element.84), channel_id=1, source_target_pairs={{0,64},{1,65},{2,66},{3,67},{4,68},{5,69},{6,70},{7,71},{8,72},{9,... | collective-permute-start | bytes 442376 | tf_op jit(solution)/shard_map/ppermute | solution.py:46
  51.9 9.9 %collective-permute-start.17 = (f16[72,1024]{1,0:T(8,128)(2,1)S(1)}, f16[72,1024]{1,0:T(8,128)(2,1)S(1)}, u32[]{:S(2)}, u32[]{:S(2)}) collective-permute-start(f16[72,1024]{1,0:T(8,128)(2,1)S(1)} %get-tuple-element.83), channel_id=1, source_target_pairs={{0,32},{1,33},{2,34},{3,35},{4,36},{5,37},{6,38},{7,39},{8,40},{9,... | collective-permute-start | bytes 442376 | tf_op jit(solution)/shard_map/ppermute | solution.py:46
  52.5 10.0 %collective-permute-start.14 = (bf16[64,1024]{1,0:T(8,128)(2,1)S(1)}, bf16[64,1024]{1,0:T(8,128)(2,1)S(1)}, u32[]{:S(2)}, u32[]{:S(2)}) collective-permute-start(bf16[64,1024]{1,0:T(8,128)(2,1)S(1)} %add_convert_fusion.1), channel_id=1, source_target_pairs={{0,96},{1,97},{2,98},{3,99},{4,100},{5,101},{6,102},{7,103},{8,104... | collective-permute-start | bytes 393224 | tf_op jit(solution)/shard_map/ppermute | solution.py:46
  57.6 8.8 %collective-permute-start.12 = (bf16[64,1024]{1,0:T(8,128)(2,1)S(1)}, bf16[64,1024]{1,0:T(8,128)(2,1)S(1)}, u32[]{:S(2)}, u32[]{:S(2)}) collective-permute-start(bf16[64,1024]{1,0:T(8,128)(2,1)S(1)} %add_convert_fusion.1), channel_id=1, source_target_pairs={{0,32},{1,33},{2,34},{3,35},{4,36},{5,37},{6,38},{7,39},{8,40},{9,... | collective-permute-start | bytes 393224 | tf_op jit(solution)/shard_map/ppermute | solution.py:46
  62.0 8.1 %collective-permute-start.20 = (f16[72,1024]{1,0:T(8,128)(2,1)S(1)}, f16[72,1024]{1,0:T(8,128)(2,1)S(1)}, u32[]{:S(2)}, u32[]{:S(2)}) collective-permute-start(f16[72,1024]{1,0:T(8,128)(2,1)S(1)} %pad_maximum_fusion.18), channel_id=1, source_target_pairs={{0,128},{1,129},{2,130},{3,131},{4,132},{5,133},{6,134},{7,135},{8... | collective-permute-start | bytes 442376 | tf_op jit(solution)/shard_map/ppermute | solution.py:46
  70.3 6.5 %collective-permute-start.23 = (bf16[64,1024]{1,0:T(8,128)(2,1)S(1)}, bf16[64,1024]{1,0:T(8,128)(2,1)S(1)}, u32[]{:S(2)}, u32[]{:S(2)}) collective-permute-start(bf16[64,1024]{1,0:T(8,128)(2,1)S(1)} %add_convert_fusion), channel_id=1, source_target_pairs={{0,96},{1,97},{2,98},{3,99},{4,100},{5,101},{6,102},{7,103},{8,104... | collective-permute-start | bytes 393224 | tf_op jit(solution)/shard_map/ppermute | solution.py:46
  70.4 6.4 %collective-permute-start.22 = (bf16[64,1024]{1,0:T(8,128)(2,1)S(1)}, bf16[64,1024]{1,0:T(8,128)(2,1)S(1)}, u32[]{:S(2)}, u32[]{:S(2)}) collective-permute-start(bf16[64,1024]{1,0:T(8,128)(2,1)S(1)} %add_convert_fusion), channel_id=1, source_target_pairs={{0,64},{1,65},{2,66},{3,67},{4,68},{5,69},{6,70},{7,71},{8,72},{9,... | collective-permute-start | bytes 393224 | tf_op jit(solution)/shard_map/ppermute | solution.py:46
  73.7 11.1 %collective-permute-start.16 = (f16[136,1536]{1,0:T(8,128)(2,1)S(1)}, f16[136,1536]{1,0:T(8,128)(2,1)S(1)}, u32[]{:S(2)}, u32[]{:S(2)}) collective-permute-start(f16[136,1536]{1,0:T(8,128)(2,1)S(1)} %pad_maximum_fusion.7), channel_id=1, source_target_pairs={{0,4},{1,5},{2,6},{3,7},{4,0},{5,1},{6,2},{7,3},{8,12},{9,13},{10,... | collective-permute-start | bytes 1253384 | tf_op jit(solution)/shard_map/ppermute | solution.py:46
  79.2 9.9 %collective-permute-start.25 = (f16[136,1536]{1,0:T(8,128)(2,1)S(1)}, f16[136,1536]{1,0:T(8,128)(2,1)S(1)}, u32[]{:S(2)}, u32[]{:S(2)}) collective-permute-start(f16[136,1536]{1,0:T(8,128)(2,1)S(1)} %get-tuple-element.82), channel_id=1, source_target_pairs={{0,12},{1,13},{2,14},{3,15},{4,8},{5,9},{6,10},{7,11},{8,4},{9,5},... | collective-permute-start | bytes 1253384 | tf_op jit(solution)/shard_map/ppermute | solution.py:46
  82.2 20.3 %collective-permute-start.24 = (f16[136,1536]{1,0:T(8,128)(2,1)S(1)}, f16[136,1536]{1,0:T(8,128)(2,1)S(1)}, u32[]{:S(2)}, u32[]{:S(2)}) collective-permute-start(f16[136,1536]{1,0:T(8,128)(2,1)S(1)} %get-tuple-element.81), channel_id=1, source_target_pairs={{0,8},{1,9},{2,10},{3,11},{4,12},{5,13},{6,14},{7,15},{8,0},{9,1},... | collective-permute-start | bytes 1253384 | tf_op jit(solution)/shard_map/ppermute | solution.py:46
  103.1 6.3 %collective-permute-start.28 = (f16[40,1536]{1,0:T(8,128)(2,1)S(1)}, f16[40,1536]{1,0:T(8,128)(2,1)S(1)}, u32[]{:S(2)}, u32[]{:S(2)}) collective-permute-start(f16[40,1536]{1,0:T(8,128)(2,1)S(1)} %get-tuple-element.80), channel_id=1, source_target_pairs={{0,3},{1,2},{2,1},{3,0},{4,7},{5,6},{6,5},{7,4},{8,11},{9,10},{10,... | collective-permute-start | bytes 368648 | tf_op jit(solution)/shard_map/ppermute | solution.py:46
  (8 other events, 40.6 us)

commit v4 on v3

--- a/solution.py
+++ b/solution.py
@@ -61,9 +61,9 @@
     return packed[:-8].astype(F32) * jnp.exp2(-e), e
 
 
-def scatter_sum(blocks, perms, e):
+def scatter_sum(blocks, perms, e, order=(1, 2, 3)):
     total, least = blocks[0], e
-    sent = [send(pack(block, e), perm) for block, perm in zip(blocks[1:], perms[1:])]
+    sent = [send(pack(blocks[k], e), perms[k]) for k in order]
     for packed in sent:
         got, its = unpack(packed)
         total, least = total + got, jnp.minimum(least, its)
@@ -219,11 +219,11 @@
     block0, block1 = product(low0)
     block2, block3 = product(low1)
     total, least = block0
-    for (block, e), k in ((block1, 1), (block2, 2), (block3, 3)):
+    for (block, e), k in ((block1, 1), (block3, 3), (block2, 2)):
         got, its = unpack(send(pack(block, e), SECOND[k]))
         total, least = total + got, jnp.minimum(least, its)
     total = total.reshape(4, half, 2 * trains)
-    total, _ = scatter_sum([total[k] for k in range(4)], FIRST, least - 2.0)
+    total, _ = scatter_sum([total[k] for k in range(4)], FIRST, least - 2.0, (3, 2, 1))
 
     kept, sent = total[:, :trains], total[:, trains:]
     got = send(sent, TO_CORE)

time: 114 us -> 112 us (0.982); the launches traced: 112 us -> 112 us
  waiting for transfers between devices: 53.5 us -> 48.8 us
  starting transfers between devices: 43.5 us -> 48 us
    ppermute x30, waiting for transfers between devices: 53.5 us -> 48.8 us  [send(): return lax.ppermute(value, BOTH, perm)]
    ppermute x30, starting transfers between devices: 43.5 us -> 48 us  [send(): return lax.ppermute(value, BOTH, perm)]
  transfers between devices with their start and end apart: 30 -> 30, of which waited for: 21 -> 20; matrix products, arithmetic and copies ran while one was open for 2% -> 2% of each run, Pallas kernels for 7% -> 7%
where the time goes in v4:
time: 112 us
  waiting for transfers between devices  48.8 us (44%)
  starting transfers between devices  48 us (43%)
  Pallas kernels  7.83 us (7%)
  other arithmetic  4.44 us (4%)
  local copies, waits for them, and re-layouts  2.54 us (2%)
    ppermute x30, waiting for transfers between devices, send(): return lax.ppermute(value, BOTH, perm)  48.8 us
    ppermute x30, starting transfers between devices, send(): return lax.ppermute(value, BOTH, perm)  48 us
    pallas_call x2, Pallas kernels, precond(): pl.pallas_call(precond_kernel, in_specs=[VMEM] * 3, out_specs=(VMEM, VMEM...  5.19 us
    pallas_call x2, Pallas kernels, scores_of(): pl.pallas_call(scores_kernel, in_specs=[VMEM] * 3, out_specs=(VMEM, VMEM)...  2.35 us
  transfers between devices with their start and end apart: 30, of which 20 were waited for; matrix products, arithmetic and copies ran while one was open for 2% of the time, Pallas kernels for 7%

profile of v4, /device:TPU:1, one launch (start us, length us, event | category | flops | bytes accessed | tf_op | source)
XLA Modules:
  0.0 112.0 jit_solution(14432743673583869541)
XLA Ops:
  0.9 3.3 %collective-permute-start = (bf16[32,1024]{1,0:T(8,128)(2,1)S(1)}, bf16[32,1024]{1,0:T(8,128)(2,1)S(1)}, u32[]{:S(2)}, u32[]{:S(2)}) collective-permute-start(bf16[32,1024]{1,0:T(8,128)(2,1)S(1)} %get-tuple-element.77), channel_id=1, source_target_pairs={{0,16},{1,17},{2,18},{3,19},{4,20},{5,21},{6,22},{7,23},{8,24},{9,... | collective-permute-start | bytes 196616 | tf_op jit(solution)/shard_map/ppermute | solution.py:46
  6.8 2.0 %collective-permute-start.1 = (bf16[32,2048]{1,0:T(8,128)(2,1)S(1)}, bf16[32,2048]{1,0:T(8,128)(2,1)S(1)}, u32[]{:S(2)}, u32[]{:S(2)}) collective-permute-start(bf16[32,2048]{1,0:T(8,128)(2,1)S(1)} %get-tuple-element.75), channel_id=1, source_target_pairs={{0,1},{1,0},{2,3},{3,2},{4,5},{5,4},{6,7},{7,6},{8,9},{9,8},{10,11... | collective-permute-start | bytes 393224 | tf_op jit(solution)/shard_map/ppermute | solution.py:46
  8.8 2.2 %copy-done.1 = f32[1024,1024]{1,0:T(8,128)S(1)} copy-done((f32[1024,1024]{1,0:T(8,128)S(1)}, f32[1024,1024]{1,0:T(8,128)}, u32[]{:S(2)}) %copy-start.1) | copy-done | bytes 4194328
  13.4 2.8 %collective-permute-start.4 = (bf16[128,2048]{1,0:T(8,128)(2,1)S(1)}, bf16[128,2048]{1,0:T(8,128)(2,1)S(1)}, u32[]{:S(2)}, u32[]{:S(2)}) collective-permute-start(bf16[128,2048]{1,0:T(8,128)(2,1)S(1)} %bitcast.85), channel_id=1, source_target_pairs={{0,12},{1,13},{2,14},{3,15},{4,8},{5,9},{6,10},{7,11},{8,4},{9,5},... | collective-permute-start | bytes 1572872 | tf_op jit(solution)/shard_map/ppermute | solution.py:46
  16.3 5.1 %collective-permute-done.5 = bf16[128,2048]{1,0:T(8,128)(2,1)S(1)} collective-permute-done((bf16[128,2048]{1,0:T(8,128)(2,1)S(1)}, bf16[128,2048]{1,0:T(8,128)(2,1)S(1)}, u32[]{:S(2)}, u32[]{:S(2)}) %collective-permute-start.5) | collective-permute-done | bytes 524320 | tf_op jit(solution)/shard_map/ppermute | solution.py:46
  21.5 2.6 %precond.2 = (f32[4,8,8,1024]{3,2,1,0:T(8,128)S(1)}, f32[8,1024]{1,0:T(8,128)S(1)}) custom-call(bf16[256,2048]{1,0:T(8,128)(2,1)S(1)} %pad_maximum_fusion.tests, f32[1024,1024]{1,0:T(8,128)S(1)} %brought_in.1.near, f32[1024,1024]{1,0:T(8,128)S(1)} %collective-permute-done.6.far), custom_call_target="tpu_custom_call" | custom-call | flops 2147483648 | bytes 8388608 | tf_op jit(solution)/shard_map/precond/pallas_call | solution.py:123
  24.1 4.3 %collective-permute-done.4 = bf16[128,2048]{1,0:T(8,128)(2,1)S(1)} collective-permute-done((bf16[128,2048]{1,0:T(8,128)(2,1)S(1)}, bf16[128,2048]{1,0:T(8,128)(2,1)S(1)}, u32[]{:S(2)}, u32[]{:S(2)}) %collective-permute-start.4) | collective-permute-done | bytes 524320 | tf_op jit(solution)/shard_map/ppermute | solution.py:46
  28.7 2.8 %collective-permute-start.9 = (f16[72,1024]{1,0:T(8,128)(2,1)S(1)}, f16[72,1024]{1,0:T(8,128)(2,1)S(1)}, u32[]{:S(2)}, u32[]{:S(2)}) collective-permute-start(f16[72,1024]{1,0:T(8,128)(2,1)S(1)} %get-tuple-element.88), channel_id=1, source_target_pairs={{0,96},{1,97},{2,98},{3,99},{4,100},{5,101},{6,102},{7,103},{8,104... | collective-permute-start | bytes 442376 | tf_op jit(solution)/shard_map/ppermute | solution.py:46
  33.2 4.5 %collective-permute-done.9 = f16[72,1024]{1,0:T(8,128)(2,1)S(1)} collective-permute-done((f16[72,1024]{1,0:T(8,128)(2,1)S(1)}, f16[72,1024]{1,0:T(8,128)(2,1)S(1)}, u32[]{:S(2)}, u32[]{:S(2)}) %collective-permute-start.9) | collective-permute-done | bytes 147488 | tf_op jit(solution)/shard_map/ppermute | solution.py:46
  40.6 2.6 %precond.3 = (f32[4,8,8,1024]{3,2,1,0:T(8,128)S(1)}, f32[8,1024]{1,0:T(8,128)S(1)}) custom-call(bf16[256,2048]{1,0:T(8,128)(2,1)S(1)} %pad_maximum_fusion.1.tests, f32[1024,1024]{1,0:T(8,128)S(1)} %brought_in.1.near, f32[1024,1024]{1,0:T(8,128)S(1)} %collective-permute-done.6.far), custom_call_target="tpu_custom_call" | custom-call | flops 2147483648 | bytes 8388608 | tf_op jit(solution)/shard_map/precond/pallas_call | solution.py:123
  43.4 5.2 %collective-permute-start.11 = (f16[72,1024]{1,0:T(8,128)(2,1)S(1)}, f16[72,1024]{1,0:T(8,128)(2,1)S(1)}, u32[]{:S(2)}, u32[]{:S(2)}) collective-permute-start(f16[72,1024]{1,0:T(8,128)(2,1)S(1)} %pad_maximum_fusion.17), channel_id=1, source_target_pairs={{0,128},{1,129},{2,130},{3,131},{4,132},{5,133},{6,134},{7,135},{8... | collective-permute-start | bytes 442376 | tf_op jit(solution)/shard_map/ppermute | solution.py:46
  48.8 2.7 %collective-permute-start.19 = (f16[72,1024]{1,0:T(8,128)(2,1)S(1)}, f16[72,1024]{1,0:T(8,128)(2,1)S(1)}, u32[]{:S(2)}, u32[]{:S(2)}) collective-permute-start(f16[72,1024]{1,0:T(8,128)(2,1)S(1)} %get-tuple-element.85), channel_id=1, source_target_pairs={{0,96},{1,97},{2,98},{3,99},{4,100},{5,101},{6,102},{7,103},{8,104... | collective-permute-start | bytes 442376 | tf_op jit(solution)/shard_map/ppermute | solution.py:46
  52.5 2.6 %collective-permute-start.14 = (bf16[64,1024]{1,0:T(8,128)(2,1)S(1)}, bf16[64,1024]{1,0:T(8,128)(2,1)S(1)}, u32[]{:S(2)}, u32[]{:S(2)}) collective-permute-start(bf16[64,1024]{1,0:T(8,128)(2,1)S(1)} %add_convert_fusion.1), channel_id=1, source_target_pairs={{0,96},{1,97},{2,98},{3,99},{4,100},{5,101},{6,102},{7,103},{8,104... | collective-permute-start | bytes 393224 | tf_op jit(solution)/shard_map/ppermute | solution.py:46
  55.1 2.5 %collective-permute-done.19 = f16[72,1024]{1,0:T(8,128)(2,1)S(1)} collective-permute-done((f16[72,1024]{1,0:T(8,128)(2,1)S(1)}, f16[72,1024]{1,0:T(8,128)(2,1)S(1)}, u32[]{:S(2)}, u32[]{:S(2)}) %collective-permute-start.19) | collective-permute-done | bytes 147488 | tf_op jit(solution)/shard_map/ppermute | solution.py:46
  57.6 4.1 %collective-permute-start.12 = (bf16[64,1024]{1,0:T(8,128)(2,1)S(1)}, bf16[64,1024]{1,0:T(8,128)(2,1)S(1)}, u32[]{:S(2)}, u32[]{:S(2)}) collective-permute-start(bf16[64,1024]{1,0:T(8,128)(2,1)S(1)} %add_convert_fusion.1), channel_id=1, source_target_pairs={{0,32},{1,33},{2,34},{3,35},{4,36},{5,37},{6,38},{7,39},{8,40},{9,... | collective-permute-start | bytes 393224 | tf_op jit(solution)/shard_map/ppermute | solution.py:46
  63.2 3.2 %collective-permute-done.12 = bf16[64,1024]{1,0:T(8,128)(2,1)S(1)} collective-permute-done((bf16[64,1024]{1,0:T(8,128)(2,1)S(1)}, bf16[64,1024]{1,0:T(8,128)(2,1)S(1)}, u32[]{:S(2)}, u32[]{:S(2)}) %collective-permute-start.12) | collective-permute-done | bytes 131104 | tf_op jit(solution)/shard_map/ppermute | solution.py:46
  68.0 2.2 %collective-permute-done.20 = f16[72,1024]{1,0:T(8,128)(2,1)S(1)} collective-permute-done((f16[72,1024]{1,0:T(8,128)(2,1)S(1)}, f16[72,1024]{1,0:T(8,128)(2,1)S(1)}, u32[]{:S(2)}, u32[]{:S(2)}) %collective-permute-start.20) | collective-permute-done | bytes 147488 | tf_op jit(solution)/shard_map/ppermute | solution.py:46
  70.4 1.8 %collective-permute-start.22 = (bf16[64,1024]{1,0:T(8,128)(2,1)S(1)}, bf16[64,1024]{1,0:T(8,128)(2,1)S(1)}, u32[]{:S(2)}, u32[]{:S(2)}) collective-permute-start(bf16[64,1024]{1,0:T(8,128)(2,1)S(1)} %add_convert_fusion), channel_id=1, source_target_pairs={{0,64},{1,65},{2,66},{3,67},{4,68},{5,69},{6,70},{7,71},{8,72},{9,... | collective-permute-start | bytes 393224 | tf_op jit(solution)/shard_map/ppermute | solution.py:46
  74.2 2.5 %collective-permute-done.23 = bf16[64,1024]{1,0:T(8,128)(2,1)S(1)} collective-permute-done((bf16[64,1024]{1,0:T(8,128)(2,1)S(1)}, bf16[64,1024]{1,0:T(8,128)(2,1)S(1)}, u32[]{:S(2)}, u32[]{:S(2)}) %collective-permute-start.23) | collective-permute-done | bytes 131104 | tf_op jit(solution)/shard_map/ppermute | solution.py:46
  79.2 5.5 %collective-permute-start.25 = (f16[136,1536]{1,0:T(8,128)(2,1)S(1)}, f16[136,1536]{1,0:T(8,128)(2,1)S(1)}, u32[]{:S(2)}, u32[]{:S(2)}) collective-permute-start(f16[136,1536]{1,0:T(8,128)(2,1)S(1)} %get-tuple-element.82), channel_id=1, source_target_pairs={{0,8},{1,9},{2,10},{3,11},{4,12},{5,13},{6,14},{7,15},{8,0},{9,1},... | collective-permute-start | bytes 1253384 | tf_op jit(solution)/shard_map/ppermute | solution.py:46
  84.7 13.6 %collective-permute-done.25 = f16[136,1536]{1,0:T(8,128)(2,1)S(1)} collective-permute-done((f16[136,1536]{1,0:T(8,128)(2,1)S(1)}, f16[136,1536]{1,0:T(8,128)(2,1)S(1)}, u32[]{:S(2)}, u32[]{:S(2)}) %collective-permute-start.25) | collective-permute-done | bytes 417824 | tf_op jit(solution)/shard_map/ppermute | solution.py:46
  99.0 2.0 %collective-permute-start.27 = (f16[40,1536]{1,0:T(8,128)(2,1)S(1)}, f16[40,1536]{1,0:T(8,128)(2,1)S(1)}, u32[]{:S(2)}, u32[]{:S(2)}) collective-permute-start(f16[40,1536]{1,0:T(8,128)(2,1)S(1)} %get-tuple-element.79), channel_id=1, source_target_pairs={{0,2},{1,3},{2,0},{3,1},{4,6},{5,7},{6,4},{7,5},{8,10},{9,11},{10,... | collective-permute-start | bytes 368648 | tf_op jit(solution)/shard_map/ppermute | solution.py:46
  101.0 1.8 %collective-permute-start.26 = (f16[40,1536]{1,0:T(8,128)(2,1)S(1)}, f16[40,1536]{1,0:T(8,128)(2,1)S(1)}, u32[]{:S(2)}, u32[]{:S(2)}) collective-permute-start(f16[40,1536]{1,0:T(8,128)(2,1)S(1)} %get-tuple-element.78), channel_id=1, source_target_pairs={{0,3},{1,2},{2,1},{3,0},{4,7},{5,6},{6,5},{7,4},{8,11},{9,10},{10,... | collective-permute-start | bytes 368648 | tf_op jit(solution)/shard_map/ppermute | solution.py:46
  106.3 4.1 %collective-permute-start.29 = (f32[32,768]{1,0:T(8,128)S(1)}, f32[32,768]{1,0:T(8,128)S(1)}, u32[]{:S(2)}, u32[]{:S(2)}) collective-permute-start(f32[32,768]{1,0:T(8,128)S(1)} %get-tuple-element.66), channel_id=1, source_target_pairs={{0,16},{1,17},{2,18},{3,19},{4,20},{5,21},{6,22},{7,23},{8,24},{9,... | collective-permute-start | bytes 294920 | tf_op jit(solution)/shard_map/ppermute | solution.py:46
  (102 shorter events, 25.6 us)
Async XLA Ops:
  5.1 16.4 %collective-permute-start.6 = (f32[1024,1024]{1,0:T(8,128)}, f32[1024,1024]{1,0:T(8,128)S(1)}, u32[]{:S(2)}, u32[]{:S(2)}) collective-permute-start(f32[1024,1024]{1,0:T(8,128)} %gram), channel_id=1, source_target_pairs={{0,16},{1,17},{2,18},{3,19},{4,20},{5,21},{6,22},{7,23},{8,24},{9,... | collective-permute-start | bytes 12582920 | tf_op jit(solution)/shard_map/ppermute | solution.py:46
  5.5 6.6 %collective-permute-start.3 = (bf16[32,2048]{1,0:T(8,128)(2,1)S(1)}, bf16[32,2048]{1,0:T(8,128)(2,1)S(1)}, u32[]{:S(2)}, u32[]{:S(2)}) collective-permute-start(bf16[32,2048]{1,0:T(8,128)(2,1)S(1)} %get-tuple-element.75), channel_id=1, source_target_pairs={{0,3},{1,2},{2,1},{3,0},{4,7},{5,6},{6,5},{7,4},{8,11},{9,10},{10,... | collective-permute-start | bytes 393224 | tf_op jit(solution)/shard_map/ppermute | solution.py:46
  6.3 5.8 %collective-permute-start.2 = (bf16[32,2048]{1,0:T(8,128)(2,1)S(1)}, bf16[32,2048]{1,0:T(8,128)(2,1)S(1)}, u32[]{:S(2)}, u32[]{:S(2)}) collective-permute-start(bf16[32,2048]{1,0:T(8,128)(2,1)S(1)} %get-tuple-element.75), channel_id=1, source_target_pairs={{0,2},{1,3},{2,0},{3,1},{4,6},{5,7},{6,4},{7,5},{8,10},{9,11},{10,... | collective-permute-start | bytes 393224 | tf_op jit(solution)/shard_map/ppermute | solution.py:46
  6.8 6.0 %collective-permute-start.1 = (bf16[32,2048]{1,0:T(8,128)(2,1)S(1)}, bf16[32,2048]{1,0:T(8,128)(2,1)S(1)}, u32[]{:S(2)}, u32[]{:S(2)}) collective-permute-start(bf16[32,2048]{1,0:T(8,128)(2,1)S(1)} %get-tuple-element.75), channel_id=1, source_target_pairs={{0,1},{1,0},{2,3},{3,2},{4,5},{5,4},{6,7},{7,6},{8,9},{9,8},{10,11... | collective-permute-start | bytes 393224 | tf_op jit(solution)/shard_map/ppermute | solution.py:46
  13.0 8.4 %collective-permute-start.5 = (bf16[128,2048]{1,0:T(8,128)(2,1)S(1)}, bf16[128,2048]{1,0:T(8,128)(2,1)S(1)}, u32[]{:S(2)}, u32[]{:S(2)}) collective-permute-start(bf16[128,2048]{1,0:T(8,128)(2,1)S(1)} %bitcast.84), channel_id=1, source_target_pairs={{0,4},{1,5},{2,6},{3,7},{4,0},{5,1},{6,2},{7,3},{8,12},{9,13},{10,... | collective-permute-start | bytes 1572872 | tf_op jit(solution)/shard_map/ppermute | solution.py:46
  13.4 15.0 %collective-permute-start.4 = (bf16[128,2048]{1,0:T(8,128)(2,1)S(1)}, bf16[128,2048]{1,0:T(8,128)(2,1)S(1)}, u32[]{:S(2)}, u32[]{:S(2)}) collective-permute-start(bf16[128,2048]{1,0:T(8,128)(2,1)S(1)} %bitcast.85), channel_id=1, source_target_pairs={{0,12},{1,13},{2,14},{3,15},{4,8},{5,9},{6,10},{7,11},{8,4},{9,5},... | collective-permute-start | bytes 1572872 | tf_op jit(solution)/shard_map/ppermute | solution.py:46
  28.7 9.0 %collective-permute-start.9 = (f16[72,1024]{1,0:T(8,128)(2,1)S(1)}, f16[72,1024]{1,0:T(8,128)(2,1)S(1)}, u32[]{:S(2)}, u32[]{:S(2)}) collective-permute-start(f16[72,1024]{1,0:T(8,128)(2,1)S(1)} %get-tuple-element.88), channel_id=1, source_target_pairs={{0,96},{1,97},{2,98},{3,99},{4,100},{5,101},{6,102},{7,103},{8,104... | collective-permute-start | bytes 442376 | tf_op jit(solution)/shard_map/ppermute | solution.py:46
  31.5 7.0 %collective-permute-start.8 = (f16[72,1024]{1,0:T(8,128)(2,1)S(1)}, f16[72,1024]{1,0:T(8,128)(2,1)S(1)}, u32[]{:S(2)}, u32[]{:S(2)}) collective-permute-start(f16[72,1024]{1,0:T(8,128)(2,1)S(1)} %get-tuple-element.87), channel_id=1, source_target_pairs={{0,64},{1,65},{2,66},{3,67},{4,68},{5,69},{6,70},{7,71},{8,72},{9,... | collective-permute-start | bytes 442376 | tf_op jit(solution)/shard_map/ppermute | solution.py:46
  31.9 7.5 %collective-permute-start.7 = (f16[72,1024]{1,0:T(8,128)(2,1)S(1)}, f16[72,1024]{1,0:T(8,128)(2,1)S(1)}, u32[]{:S(2)}, u32[]{:S(2)}) collective-permute-start(f16[72,1024]{1,0:T(8,128)(2,1)S(1)} %get-tuple-element.86), channel_id=1, source_target_pairs={{0,32},{1,33},{2,34},{3,35},{4,36},{5,37},{6,38},{7,39},{8,40},{9,... | collective-permute-start | bytes 442376 | tf_op jit(solution)/shard_map/ppermute | solution.py:46
  32.2 8.3 %collective-permute-start.10 = (bf16[128,2048]{1,0:T(8,128)(2,1)S(1)}, bf16[128,2048]{1,0:T(8,128)(2,1)S(1)}, u32[]{:S(2)}, u32[]{:S(2)}) collective-permute-start(bf16[128,2048]{1,0:T(8,128)(2,1)S(1)} %collective-permute-done.4), channel_id=1, source_target_pairs={{0,4},{1,5},{2,6},{3,7},{4,0},{5,1},{6,2},{7,3},{8,12},{9,13},{10,... | collective-permute-start | bytes 1572872 | tf_op jit(solution)/shard_map/ppermute | solution.py:46
  32.7 33.8 %collective-permute-start.15 = (bf16[768,1024]{1,0:T(8,128)(2,1)S(1)}, bf16[768,1024]{1,0:T(8,128)(2,1)S(1)}, u32[]{:S(2)}, u32[]{:S(2)}) collective-permute-start(bf16[768,1024]{1,0:T(8,128)(2,1)S(1)} %copy-done), channel_id=1, source_target_pairs={{0,16},{1,17},{2,18},{3,19},{4,20},{5,21},{6,22},{7,23},{8,24},{9,... | collective-permute-start | bytes 4718600 | tf_op jit(solution)/shard_map/ppermute | solution.py:46
  43.4 9.1 %collective-permute-start.11 = (f16[72,1024]{1,0:T(8,128)(2,1)S(1)}, f16[72,1024]{1,0:T(8,128)(2,1)S(1)}, u32[]{:S(2)}, u32[]{:S(2)}) collective-permute-start(f16[72,1024]{1,0:T(8,128)(2,1)S(1)} %pad_maximum_fusion.17), channel_id=1, source_target_pairs={{0,128},{1,129},{2,130},{3,131},{4,132},{5,133},{6,134},{7,135},{8... | collective-permute-start | bytes 442376 | tf_op jit(solution)/shard_map/ppermute | solution.py:46
  48.8 8.8 %collective-permute-start.19 = (f16[72,1024]{1,0:T(8,128)(2,1)S(1)}, f16[72,1024]{1,0:T(8,128)(2,1)S(1)}, u32[]{:S(2)}, u32[]{:S(2)}) collective-permute-start(f16[72,1024]{1,0:T(8,128)(2,1)S(1)} %get-tuple-element.85), channel_id=1, source_target_pairs={{0,96},{1,97},{2,98},{3,99},{4,100},{5,101},{6,102},{7,103},{8,104... | collective-permute-start | bytes 442376 | tf_op jit(solution)/shard_map/ppermute | solution.py:46
  51.5 6.1 %collective-permute-start.18 = (f16[72,1024]{1,0:T(8,128)(2,1)S(1)}, f16[72,1024]{1,0:T(8,128)(2,1)S(1)}, u32[]{:S(2)}, u32[]{:S(2)}) collective-permute-start(f16[72,1024]{1,0:T(8,128)(2,1)S(1)} %get-tuple-element.84), channel_id=1, source_target_pairs={{0,64},{1,65},{2,66},{3,67},{4,68},{5,69},{6,70},{7,71},{8,72},{9,... | collective-permute-start | bytes 442376 | tf_op jit(solution)/shard_map/ppermute | solution.py:46
  51.9 9.9 %collective-permute-start.17 = (f16[72,1024]{1,0:T(8,128)(2,1)S(1)}, f16[72,1024]{1,0:T(8,128)(2,1)S(1)}, u32[]{:S(2)}, u32[]{:S(2)}) collective-permute-start(f16[72,1024]{1,0:T(8,128)(2,1)S(1)} %get-tuple-element.83), channel_id=1, source_target_pairs={{0,32},{1,33},{2,34},{3,35},{4,36},{5,37},{6,38},{7,39},{8,40},{9,... | collective-permute-start | bytes 442376 | tf_op jit(solution)/shard_map/ppermute | solution.py:46
  52.5 10.0 %collective-permute-start.14 = (bf16[64,1024]{1,0:T(8,128)(2,1)S(1)}, bf16[64,1024]{1,0:T(8,128)(2,1)S(1)}, u32[]{:S(2)}, u32[]{:S(2)}) collective-permute-start(bf16[64,1024]{1,0:T(8,128)(2,1)S(1)} %add_convert_fusion.1), channel_id=1, source_target_pairs={{0,96},{1,97},{2,98},{3,99},{4,100},{5,101},{6,102},{7,103},{8,104... | collective-permute-start | bytes 393224 | tf_op jit(solution)/shard_map/ppermute | solution.py:46
  57.6 8.8 %collective-permute-start.12 = (bf16[64,1024]{1,0:T(8,128)(2,1)S(1)}, bf16[64,1024]{1,0:T(8,128)(2,1)S(1)}, u32[]{:S(2)}, u32[]{:S(2)}) collective-permute-start(bf16[64,1024]{1,0:T(8,128)(2,1)S(1)} %add_convert_fusion.1), channel_id=1, source_target_pairs={{0,32},{1,33},{2,34},{3,35},{4,36},{5,37},{6,38},{7,39},{8,40},{9,... | collective-permute-start | bytes 393224 | tf_op jit(solution)/shard_map/ppermute | solution.py:46
  62.0 8.1 %collective-permute-start.20 = (f16[72,1024]{1,0:T(8,128)(2,1)S(1)}, f16[72,1024]{1,0:T(8,128)(2,1)S(1)}, u32[]{:S(2)}, u32[]{:S(2)}) collective-permute-start(f16[72,1024]{1,0:T(8,128)(2,1)S(1)} %pad_maximum_fusion.18), channel_id=1, source_target_pairs={{0,128},{1,129},{2,130},{3,131},{4,132},{5,133},{6,134},{7,135},{8... | collective-permute-start | bytes 442376 | tf_op jit(solution)/shard_map/ppermute | solution.py:46
  70.3 6.5 %collective-permute-start.23 = (bf16[64,1024]{1,0:T(8,128)(2,1)S(1)}, bf16[64,1024]{1,0:T(8,128)(2,1)S(1)}, u32[]{:S(2)}, u32[]{:S(2)}) collective-permute-start(bf16[64,1024]{1,0:T(8,128)(2,1)S(1)} %add_convert_fusion), channel_id=1, source_target_pairs={{0,96},{1,97},{2,98},{3,99},{4,100},{5,101},{6,102},{7,103},{8,104... | collective-permute-start | bytes 393224 | tf_op jit(solution)/shard_map/ppermute | solution.py:46
  70.4 6.4 %collective-permute-start.22 = (bf16[64,1024]{1,0:T(8,128)(2,1)S(1)}, bf16[64,1024]{1,0:T(8,128)(2,1)S(1)}, u32[]{:S(2)}, u32[]{:S(2)}) collective-permute-start(bf16[64,1024]{1,0:T(8,128)(2,1)S(1)} %add_convert_fusion), channel_id=1, source_target_pairs={{0,64},{1,65},{2,66},{3,67},{4,68},{5,69},{6,70},{7,71},{8,72},{9,... | collective-permute-start | bytes 393224 | tf_op jit(solution)/shard_map/ppermute | solution.py:46
  73.7 11.0 %collective-permute-start.16 = (f16[136,1536]{1,0:T(8,128)(2,1)S(1)}, f16[136,1536]{1,0:T(8,128)(2,1)S(1)}, u32[]{:S(2)}, u32[]{:S(2)}) collective-permute-start(f16[136,1536]{1,0:T(8,128)(2,1)S(1)} %pad_maximum_fusion.7), channel_id=1, source_target_pairs={{0,4},{1,5},{2,6},{3,7},{4,0},{5,1},{6,2},{7,3},{8,12},{9,13},{10,... | collective-permute-start | bytes 1253384 | tf_op jit(solution)/shard_map/ppermute | solution.py:46
  79.2 19.1 %collective-permute-start.25 = (f16[136,1536]{1,0:T(8,128)(2,1)S(1)}, f16[136,1536]{1,0:T(8,128)(2,1)S(1)}, u32[]{:S(2)}, u32[]{:S(2)}) collective-permute-start(f16[136,1536]{1,0:T(8,128)(2,1)S(1)} %get-tuple-element.82), channel_id=1, source_target_pairs={{0,8},{1,9},{2,10},{3,11},{4,12},{5,13},{6,14},{7,15},{8,0},{9,1},... | collective-permute-start | bytes 1253384 | tf_op jit(solution)/shard_map/ppermute | solution.py:46
  84.7 13.6 %collective-permute-start.24 = (f16[136,1536]{1,0:T(8,128)(2,1)S(1)}, f16[136,1536]{1,0:T(8,128)(2,1)S(1)}, u32[]{:S(2)}, u32[]{:S(2)}) collective-permute-start(f16[136,1536]{1,0:T(8,128)(2,1)S(1)} %get-tuple-element.81), channel_id=1, source_target_pairs={{0,12},{1,13},{2,14},{3,15},{4,8},{5,9},{6,10},{7,11},{8,4},{9,5},... | collective-permute-start | bytes 1253384 | tf_op jit(solution)/shard_map/ppermute | solution.py:46
  99.0 5.6 %collective-permute-start.27 = (f16[40,1536]{1,0:T(8,128)(2,1)S(1)}, f16[40,1536]{1,0:T(8,128)(2,1)S(1)}, u32[]{:S(2)}, u32[]{:S(2)}) collective-permute-start(f16[40,1536]{1,0:T(8,128)(2,1)S(1)} %get-tuple-element.79), channel_id=1, source_target_pairs={{0,2},{1,3},{2,0},{3,1},{4,6},{5,7},{6,4},{7,5},{8,10},{9,11},{10,... | collective-permute-start | bytes 368648 | tf_op jit(solution)/shard_map/ppermute | solution.py:46
  (8 other events, 42.5 us)

commit v5 on v4

--- a/solution.py
+++ b/solution.py
@@ -191,7 +191,7 @@
     block = gather(block, FIRST).reshape(4 * half, 2 * width)
     near = brought_in(inverse_gram)
     block, near = lax.optimization_barrier((block, near))
-    slot1, slot3 = send(block, SECOND[1]), send(block, SECOND[3])
+    slot3, slot1 = send(block, SECOND[3]), send(block, SECOND[1])
     part = precond(jnp.concatenate([block, slot1]), near, far_gram)
     slot3, part = lax.optimization_barrier((slot3, part))
     slot2 = send(slot3, SECOND[1])

time: 112 us -> 112 us (level)
  no operation moved by 1% of the time
where the time goes in v5:
time: 112 us
  waiting for transfers between devices  48.8 us (44%)
  starting transfers between devices  48 us (43%)
  Pallas kernels  7.83 us (7%)
  other arithmetic  4.44 us (4%)
  local copies, waits for them, and re-layouts  2.54 us (2%)
    ppermute x30, waiting for transfers between devices, send(): return lax.ppermute(value, BOTH, perm)  48.8 us
    ppermute x30, starting transfers between devices, send(): return lax.ppermute(value, BOTH, perm)  48 us
    pallas_call x2, Pallas kernels, precond(): pl.pallas_call(precond_kernel, in_specs=[VMEM] * 3, out_specs=(VMEM, VMEM...  5.19 us
    pallas_call x2, Pallas kernels, scores_of(): pl.pallas_call(scores_kernel, in_specs=[VMEM] * 3, out_specs=(VMEM, VMEM)...  2.35 us
  transfers between devices with their start and end apart: 30, of which 20 were waited for; matrix products, arithmetic and copies ran while one was open for 2% of the time, Pallas kernels for 7%

profile of v5, /device:TPU:1, one launch (start us, length us, event | category | flops | bytes accessed | tf_op | source)
XLA Modules:
  0.0 112.0 jit_solution(14432743673583869541)
XLA Ops:
  0.9 3.3 %collective-permute-start = (bf16[32,1024]{1,0:T(8,128)(2,1)S(1)}, bf16[32,1024]{1,0:T(8,128)(2,1)S(1)}, u32[]{:S(2)}, u32[]{:S(2)}) collective-permute-start(bf16[32,1024]{1,0:T(8,128)(2,1)S(1)} %get-tuple-element.77), channel_id=1, source_target_pairs={{0,16},{1,17},{2,18},{3,19},{4,20},{5,21},{6,22},{7,23},{8,24},{9,... | collective-permute-start | bytes 196616 | tf_op jit(solution)/shard_map/ppermute | solution.py:46
  6.8 2.0 %collective-permute-start.1 = (bf16[32,2048]{1,0:T(8,128)(2,1)S(1)}, bf16[32,2048]{1,0:T(8,128)(2,1)S(1)}, u32[]{:S(2)}, u32[]{:S(2)}) collective-permute-start(bf16[32,2048]{1,0:T(8,128)(2,1)S(1)} %get-tuple-element.75), channel_id=1, source_target_pairs={{0,1},{1,0},{2,3},{3,2},{4,5},{5,4},{6,7},{7,6},{8,9},{9,8},{10,11... | collective-permute-start | bytes 393224 | tf_op jit(solution)/shard_map/ppermute | solution.py:46
  8.8 2.2 %copy-done.1 = f32[1024,1024]{1,0:T(8,128)S(1)} copy-done((f32[1024,1024]{1,0:T(8,128)S(1)}, f32[1024,1024]{1,0:T(8,128)}, u32[]{:S(2)}) %copy-start.1) | copy-done | bytes 4194328
  13.4 2.8 %collective-permute-start.4 = (bf16[128,2048]{1,0:T(8,128)(2,1)S(1)}, bf16[128,2048]{1,0:T(8,128)(2,1)S(1)}, u32[]{:S(2)}, u32[]{:S(2)}) collective-permute-start(bf16[128,2048]{1,0:T(8,128)(2,1)S(1)} %bitcast.85), channel_id=1, source_target_pairs={{0,12},{1,13},{2,14},{3,15},{4,8},{5,9},{6,10},{7,11},{8,4},{9,5},... | collective-permute-start | bytes 1572872 | tf_op jit(solution)/shard_map/ppermute | solution.py:46
  16.3 5.1 %collective-permute-done.5 = bf16[128,2048]{1,0:T(8,128)(2,1)S(1)} collective-permute-done((bf16[128,2048]{1,0:T(8,128)(2,1)S(1)}, bf16[128,2048]{1,0:T(8,128)(2,1)S(1)}, u32[]{:S(2)}, u32[]{:S(2)}) %collective-permute-start.5) | collective-permute-done | bytes 524320 | tf_op jit(solution)/shard_map/ppermute | solution.py:46
  21.5 2.6 %precond.2 = (f32[4,8,8,1024]{3,2,1,0:T(8,128)S(1)}, f32[8,1024]{1,0:T(8,128)S(1)}) custom-call(bf16[256,2048]{1,0:T(8,128)(2,1)S(1)} %pad_maximum_fusion.tests, f32[1024,1024]{1,0:T(8,128)S(1)} %brought_in.1.near, f32[1024,1024]{1,0:T(8,128)S(1)} %collective-permute-done.6.far), custom_call_target="tpu_custom_call" | custom-call | flops 2147483648 | bytes 8388608 | tf_op jit(solution)/shard_map/precond/pallas_call | solution.py:123
  24.1 4.3 %collective-permute-done.4 = bf16[128,2048]{1,0:T(8,128)(2,1)S(1)} collective-permute-done((bf16[128,2048]{1,0:T(8,128)(2,1)S(1)}, bf16[128,2048]{1,0:T(8,128)(2,1)S(1)}, u32[]{:S(2)}, u32[]{:S(2)}) %collective-permute-start.4) | collective-permute-done | bytes 524320 | tf_op jit(solution)/shard_map/ppermute | solution.py:46
  28.7 2.8 %collective-permute-start.9 = (f16[72,1024]{1,0:T(8,128)(2,1)S(1)}, f16[72,1024]{1,0:T(8,128)(2,1)S(1)}, u32[]{:S(2)}, u32[]{:S(2)}) collective-permute-start(f16[72,1024]{1,0:T(8,128)(2,1)S(1)} %get-tuple-element.88), channel_id=1, source_target_pairs={{0,96},{1,97},{2,98},{3,99},{4,100},{5,101},{6,102},{7,103},{8,104... | collective-permute-start | bytes 442376 | tf_op jit(solution)/shard_map/ppermute | solution.py:46
  33.2 4.5 %collective-permute-done.9 = f16[72,1024]{1,0:T(8,128)(2,1)S(1)} collective-permute-done((f16[72,1024]{1,0:T(8,128)(2,1)S(1)}, f16[72,1024]{1,0:T(8,128)(2,1)S(1)}, u32[]{:S(2)}, u32[]{:S(2)}) %collective-permute-start.9) | collective-permute-done | bytes 147488 | tf_op jit(solution)/shard_map/ppermute | solution.py:46
  40.6 2.6 %precond.3 = (f32[4,8,8,1024]{3,2,1,0:T(8,128)S(1)}, f32[8,1024]{1,0:T(8,128)S(1)}) custom-call(bf16[256,2048]{1,0:T(8,128)(2,1)S(1)} %pad_maximum_fusion.1.tests, f32[1024,1024]{1,0:T(8,128)S(1)} %brought_in.1.near, f32[1024,1024]{1,0:T(8,128)S(1)} %collective-permute-done.6.far), custom_call_target="tpu_custom_call" | custom-call | flops 2147483648 | bytes 8388608 | tf_op jit(solution)/shard_map/precond/pallas_call | solution.py:123
  43.4 5.2 %collective-permute-start.11 = (f16[72,1024]{1,0:T(8,128)(2,1)S(1)}, f16[72,1024]{1,0:T(8,128)(2,1)S(1)}, u32[]{:S(2)}, u32[]{:S(2)}) collective-permute-start(f16[72,1024]{1,0:T(8,128)(2,1)S(1)} %pad_maximum_fusion.17), channel_id=1, source_target_pairs={{0,128},{1,129},{2,130},{3,131},{4,132},{5,133},{6,134},{7,135},{8... | collective-permute-start | bytes 442376 | tf_op jit(solution)/shard_map/ppermute | solution.py:46
  48.8 2.7 %collective-permute-start.19 = (f16[72,1024]{1,0:T(8,128)(2,1)S(1)}, f16[72,1024]{1,0:T(8,128)(2,1)S(1)}, u32[]{:S(2)}, u32[]{:S(2)}) collective-permute-start(f16[72,1024]{1,0:T(8,128)(2,1)S(1)} %get-tuple-element.85), channel_id=1, source_target_pairs={{0,96},{1,97},{2,98},{3,99},{4,100},{5,101},{6,102},{7,103},{8,104... | collective-permute-start | bytes 442376 | tf_op jit(solution)/shard_map/ppermute | solution.py:46
  52.5 2.6 %collective-permute-start.14 = (bf16[64,1024]{1,0:T(8,128)(2,1)S(1)}, bf16[64,1024]{1,0:T(8,128)(2,1)S(1)}, u32[]{:S(2)}, u32[]{:S(2)}) collective-permute-start(bf16[64,1024]{1,0:T(8,128)(2,1)S(1)} %add_convert_fusion.1), channel_id=1, source_target_pairs={{0,96},{1,97},{2,98},{3,99},{4,100},{5,101},{6,102},{7,103},{8,104... | collective-permute-start | bytes 393224 | tf_op jit(solution)/shard_map/ppermute | solution.py:46
  55.1 2.5 %collective-permute-done.19 = f16[72,1024]{1,0:T(8,128)(2,1)S(1)} collective-permute-done((f16[72,1024]{1,0:T(8,128)(2,1)S(1)}, f16[72,1024]{1,0:T(8,128)(2,1)S(1)}, u32[]{:S(2)}, u32[]{:S(2)}) %collective-permute-start.19) | collective-permute-done | bytes 147488 | tf_op jit(solution)/shard_map/ppermute | solution.py:46
  57.6 4.1 %collective-permute-start.12 = (bf16[64,1024]{1,0:T(8,128)(2,1)S(1)}, bf16[64,1024]{1,0:T(8,128)(2,1)S(1)}, u32[]{:S(2)}, u32[]{:S(2)}) collective-permute-start(bf16[64,1024]{1,0:T(8,128)(2,1)S(1)} %add_convert_fusion.1), channel_id=1, source_target_pairs={{0,32},{1,33},{2,34},{3,35},{4,36},{5,37},{6,38},{7,39},{8,40},{9,... | collective-permute-start | bytes 393224 | tf_op jit(solution)/shard_map/ppermute | solution.py:46
  63.2 3.2 %collective-permute-done.12 = bf16[64,1024]{1,0:T(8,128)(2,1)S(1)} collective-permute-done((bf16[64,1024]{1,0:T(8,128)(2,1)S(1)}, bf16[64,1024]{1,0:T(8,128)(2,1)S(1)}, u32[]{:S(2)}, u32[]{:S(2)}) %collective-permute-start.12) | collective-permute-done | bytes 131104 | tf_op jit(solution)/shard_map/ppermute | solution.py:46
  68.0 2.2 %collective-permute-done.20 = f16[72,1024]{1,0:T(8,128)(2,1)S(1)} collective-permute-done((f16[72,1024]{1,0:T(8,128)(2,1)S(1)}, f16[72,1024]{1,0:T(8,128)(2,1)S(1)}, u32[]{:S(2)}, u32[]{:S(2)}) %collective-permute-start.20) | collective-permute-done | bytes 147488 | tf_op jit(solution)/shard_map/ppermute | solution.py:46
  70.4 1.8 %collective-permute-start.22 = (bf16[64,1024]{1,0:T(8,128)(2,1)S(1)}, bf16[64,1024]{1,0:T(8,128)(2,1)S(1)}, u32[]{:S(2)}, u32[]{:S(2)}) collective-permute-start(bf16[64,1024]{1,0:T(8,128)(2,1)S(1)} %add_convert_fusion), channel_id=1, source_target_pairs={{0,64},{1,65},{2,66},{3,67},{4,68},{5,69},{6,70},{7,71},{8,72},{9,... | collective-permute-start | bytes 393224 | tf_op jit(solution)/shard_map/ppermute | solution.py:46
  74.2 2.5 %collective-permute-done.23 = bf16[64,1024]{1,0:T(8,128)(2,1)S(1)} collective-permute-done((bf16[64,1024]{1,0:T(8,128)(2,1)S(1)}, bf16[64,1024]{1,0:T(8,128)(2,1)S(1)}, u32[]{:S(2)}, u32[]{:S(2)}) %collective-permute-start.23) | collective-permute-done | bytes 131104 | tf_op jit(solution)/shard_map/ppermute | solution.py:46
  79.2 5.5 %collective-permute-start.25 = (f16[136,1536]{1,0:T(8,128)(2,1)S(1)}, f16[136,1536]{1,0:T(8,128)(2,1)S(1)}, u32[]{:S(2)}, u32[]{:S(2)}) collective-permute-start(f16[136,1536]{1,0:T(8,128)(2,1)S(1)} %get-tuple-element.82), channel_id=1, source_target_pairs={{0,8},{1,9},{2,10},{3,11},{4,12},{5,13},{6,14},{7,15},{8,0},{9,1},... | collective-permute-start | bytes 1253384 | tf_op jit(solution)/shard_map/ppermute | solution.py:46
  84.7 13.6 %collective-permute-done.25 = f16[136,1536]{1,0:T(8,128)(2,1)S(1)} collective-permute-done((f16[136,1536]{1,0:T(8,128)(2,1)S(1)}, f16[136,1536]{1,0:T(8,128)(2,1)S(1)}, u32[]{:S(2)}, u32[]{:S(2)}) %collective-permute-start.25) | collective-permute-done | bytes 417824 | tf_op jit(solution)/shard_map/ppermute | solution.py:46
  99.0 2.0 %collective-permute-start.27 = (f16[40,1536]{1,0:T(8,128)(2,1)S(1)}, f16[40,1536]{1,0:T(8,128)(2,1)S(1)}, u32[]{:S(2)}, u32[]{:S(2)}) collective-permute-start(f16[40,1536]{1,0:T(8,128)(2,1)S(1)} %get-tuple-element.79), channel_id=1, source_target_pairs={{0,2},{1,3},{2,0},{3,1},{4,6},{5,7},{6,4},{7,5},{8,10},{9,11},{10,... | collective-permute-start | bytes 368648 | tf_op jit(solution)/shard_map/ppermute | solution.py:46
  101.0 1.8 %collective-permute-start.26 = (f16[40,1536]{1,0:T(8,128)(2,1)S(1)}, f16[40,1536]{1,0:T(8,128)(2,1)S(1)}, u32[]{:S(2)}, u32[]{:S(2)}) collective-permute-start(f16[40,1536]{1,0:T(8,128)(2,1)S(1)} %get-tuple-element.78), channel_id=1, source_target_pairs={{0,3},{1,2},{2,1},{3,0},{4,7},{5,6},{6,5},{7,4},{8,11},{9,10},{10,... | collective-permute-start | bytes 368648 | tf_op jit(solution)/shard_map/ppermute | solution.py:46
  106.3 4.1 %collective-permute-start.29 = (f32[32,768]{1,0:T(8,128)S(1)}, f32[32,768]{1,0:T(8,128)S(1)}, u32[]{:S(2)}, u32[]{:S(2)}) collective-permute-start(f32[32,768]{1,0:T(8,128)S(1)} %get-tuple-element.66), channel_id=1, source_target_pairs={{0,16},{1,17},{2,18},{3,19},{4,20},{5,21},{6,22},{7,23},{8,24},{9,... | collective-permute-start | bytes 294920 | tf_op jit(solution)/shard_map/ppermute | solution.py:46
  (102 shorter events, 25.6 us)
Async XLA Ops:
  5.1 16.4 %collective-permute-start.6 = (f32[1024,1024]{1,0:T(8,128)}, f32[1024,1024]{1,0:T(8,128)S(1)}, u32[]{:S(2)}, u32[]{:S(2)}) collective-permute-start(f32[1024,1024]{1,0:T(8,128)} %gram), channel_id=1, source_target_pairs={{0,16},{1,17},{2,18},{3,19},{4,20},{5,21},{6,22},{7,23},{8,24},{9,... | collective-permute-start | bytes 12582920 | tf_op jit(solution)/shard_map/ppermute | solution.py:46
  5.5 6.6 %collective-permute-start.3 = (bf16[32,2048]{1,0:T(8,128)(2,1)S(1)}, bf16[32,2048]{1,0:T(8,128)(2,1)S(1)}, u32[]{:S(2)}, u32[]{:S(2)}) collective-permute-start(bf16[32,2048]{1,0:T(8,128)(2,1)S(1)} %get-tuple-element.75), channel_id=1, source_target_pairs={{0,3},{1,2},{2,1},{3,0},{4,7},{5,6},{6,5},{7,4},{8,11},{9,10},{10,... | collective-permute-start | bytes 393224 | tf_op jit(solution)/shard_map/ppermute | solution.py:46
  6.3 5.8 %collective-permute-start.2 = (bf16[32,2048]{1,0:T(8,128)(2,1)S(1)}, bf16[32,2048]{1,0:T(8,128)(2,1)S(1)}, u32[]{:S(2)}, u32[]{:S(2)}) collective-permute-start(bf16[32,2048]{1,0:T(8,128)(2,1)S(1)} %get-tuple-element.75), channel_id=1, source_target_pairs={{0,2},{1,3},{2,0},{3,1},{4,6},{5,7},{6,4},{7,5},{8,10},{9,11},{10,... | collective-permute-start | bytes 393224 | tf_op jit(solution)/shard_map/ppermute | solution.py:46
  6.8 6.0 %collective-permute-start.1 = (bf16[32,2048]{1,0:T(8,128)(2,1)S(1)}, bf16[32,2048]{1,0:T(8,128)(2,1)S(1)}, u32[]{:S(2)}, u32[]{:S(2)}) collective-permute-start(bf16[32,2048]{1,0:T(8,128)(2,1)S(1)} %get-tuple-element.75), channel_id=1, source_target_pairs={{0,1},{1,0},{2,3},{3,2},{4,5},{5,4},{6,7},{7,6},{8,9},{9,8},{10,11... | collective-permute-start | bytes 393224 | tf_op jit(solution)/shard_map/ppermute | solution.py:46
  13.0 8.4 %collective-permute-start.5 = (bf16[128,2048]{1,0:T(8,128)(2,1)S(1)}, bf16[128,2048]{1,0:T(8,128)(2,1)S(1)}, u32[]{:S(2)}, u32[]{:S(2)}) collective-permute-start(bf16[128,2048]{1,0:T(8,128)(2,1)S(1)} %bitcast.84), channel_id=1, source_target_pairs={{0,4},{1,5},{2,6},{3,7},{4,0},{5,1},{6,2},{7,3},{8,12},{9,13},{10,... | collective-permute-start | bytes 1572872 | tf_op jit(solution)/shard_map/ppermute | solution.py:46
  13.4 15.0 %collective-permute-start.4 = (bf16[128,2048]{1,0:T(8,128)(2,1)S(1)}, bf16[128,2048]{1,0:T(8,128)(2,1)S(1)}, u32[]{:S(2)}, u32[]{:S(2)}) collective-permute-start(bf16[128,2048]{1,0:T(8,128)(2,1)S(1)} %bitcast.85), channel_id=1, source_target_pairs={{0,12},{1,13},{2,14},{3,15},{4,8},{5,9},{6,10},{7,11},{8,4},{9,5},... | collective-permute-start | bytes 1572872 | tf_op jit(solution)/shard_map/ppermute | solution.py:46
  28.7 9.0 %collective-permute-start.9 = (f16[72,1024]{1,0:T(8,128)(2,1)S(1)}, f16[72,1024]{1,0:T(8,128)(2,1)S(1)}, u32[]{:S(2)}, u32[]{:S(2)}) collective-permute-start(f16[72,1024]{1,0:T(8,128)(2,1)S(1)} %get-tuple-element.88), channel_id=1, source_target_pairs={{0,96},{1,97},{2,98},{3,99},{4,100},{5,101},{6,102},{7,103},{8,104... | collective-permute-start | bytes 442376 | tf_op jit(solution)/shard_map/ppermute | solution.py:46
  31.5 7.0 %collective-permute-start.8 = (f16[72,1024]{1,0:T(8,128)(2,1)S(1)}, f16[72,1024]{1,0:T(8,128)(2,1)S(1)}, u32[]{:S(2)}, u32[]{:S(2)}) collective-permute-start(f16[72,1024]{1,0:T(8,128)(2,1)S(1)} %get-tuple-element.87), channel_id=1, source_target_pairs={{0,64},{1,65},{2,66},{3,67},{4,68},{5,69},{6,70},{7,71},{8,72},{9,... | collective-permute-start | bytes 442376 | tf_op jit(solution)/shard_map/ppermute | solution.py:46
  31.9 7.5 %collective-permute-start.7 = (f16[72,1024]{1,0:T(8,128)(2,1)S(1)}, f16[72,1024]{1,0:T(8,128)(2,1)S(1)}, u32[]{:S(2)}, u32[]{:S(2)}) collective-permute-start(f16[72,1024]{1,0:T(8,128)(2,1)S(1)} %get-tuple-element.86), channel_id=1, source_target_pairs={{0,32},{1,33},{2,34},{3,35},{4,36},{5,37},{6,38},{7,39},{8,40},{9,... | collective-permute-start | bytes 442376 | tf_op jit(solution)/shard_map/ppermute | solution.py:46
  32.2 8.3 %collective-permute-start.10 = (bf16[128,2048]{1,0:T(8,128)(2,1)S(1)}, bf16[128,2048]{1,0:T(8,128)(2,1)S(1)}, u32[]{:S(2)}, u32[]{:S(2)}) collective-permute-start(bf16[128,2048]{1,0:T(8,128)(2,1)S(1)} %collective-permute-done.4), channel_id=1, source_target_pairs={{0,4},{1,5},{2,6},{3,7},{4,0},{5,1},{6,2},{7,3},{8,12},{9,13},{10,... | collective-permute-start | bytes 1572872 | tf_op jit(solution)/shard_map/ppermute | solution.py:46
  32.7 33.8 %collective-permute-start.15 = (bf16[768,1024]{1,0:T(8,128)(2,1)S(1)}, bf16[768,1024]{1,0:T(8,128)(2,1)S(1)}, u32[]{:S(2)}, u32[]{:S(2)}) collective-permute-start(bf16[768,1024]{1,0:T(8,128)(2,1)S(1)} %copy-done), channel_id=1, source_target_pairs={{0,16},{1,17},{2,18},{3,19},{4,20},{5,21},{6,22},{7,23},{8,24},{9,... | collective-permute-start | bytes 4718600 | tf_op jit(solution)/shard_map/ppermute | solution.py:46
  43.4 9.1 %collective-permute-start.11 = (f16[72,1024]{1,0:T(8,128)(2,1)S(1)}, f16[72,1024]{1,0:T(8,128)(2,1)S(1)}, u32[]{:S(2)}, u32[]{:S(2)}) collective-permute-start(f16[72,1024]{1,0:T(8,128)(2,1)S(1)} %pad_maximum_fusion.17), channel_id=1, source_target_pairs={{0,128},{1,129},{2,130},{3,131},{4,132},{5,133},{6,134},{7,135},{8... | collective-permute-start | bytes 442376 | tf_op jit(solution)/shard_map/ppermute | solution.py:46
  48.8 8.8 %collective-permute-start.19 = (f16[72,1024]{1,0:T(8,128)(2,1)S(1)}, f16[72,1024]{1,0:T(8,128)(2,1)S(1)}, u32[]{:S(2)}, u32[]{:S(2)}) collective-permute-start(f16[72,1024]{1,0:T(8,128)(2,1)S(1)} %get-tuple-element.85), channel_id=1, source_target_pairs={{0,96},{1,97},{2,98},{3,99},{4,100},{5,101},{6,102},{7,103},{8,104... | collective-permute-start | bytes 442376 | tf_op jit(solution)/shard_map/ppermute | solution.py:46
  51.5 6.1 %collective-permute-start.18 = (f16[72,1024]{1,0:T(8,128)(2,1)S(1)}, f16[72,1024]{1,0:T(8,128)(2,1)S(1)}, u32[]{:S(2)}, u32[]{:S(2)}) collective-permute-start(f16[72,1024]{1,0:T(8,128)(2,1)S(1)} %get-tuple-element.84), channel_id=1, source_target_pairs={{0,64},{1,65},{2,66},{3,67},{4,68},{5,69},{6,70},{7,71},{8,72},{9,... | collective-permute-start | bytes 442376 | tf_op jit(solution)/shard_map/ppermute | solution.py:46
  51.9 9.9 %collective-permute-start.17 = (f16[72,1024]{1,0:T(8,128)(2,1)S(1)}, f16[72,1024]{1,0:T(8,128)(2,1)S(1)}, u32[]{:S(2)}, u32[]{:S(2)}) collective-permute-start(f16[72,1024]{1,0:T(8,128)(2,1)S(1)} %get-tuple-element.83), channel_id=1, source_target_pairs={{0,32},{1,33},{2,34},{3,35},{4,36},{5,37},{6,38},{7,39},{8,40},{9,... | collective-permute-start | bytes 442376 | tf_op jit(solution)/shard_map/ppermute | solution.py:46
  52.5 10.0 %collective-permute-start.14 = (bf16[64,1024]{1,0:T(8,128)(2,1)S(1)}, bf16[64,1024]{1,0:T(8,128)(2,1)S(1)}, u32[]{:S(2)}, u32[]{:S(2)}) collective-permute-start(bf16[64,1024]{1,0:T(8,128)(2,1)S(1)} %add_convert_fusion.1), channel_id=1, source_target_pairs={{0,96},{1,97},{2,98},{3,99},{4,100},{5,101},{6,102},{7,103},{8,104... | collective-permute-start | bytes 393224 | tf_op jit(solution)/shard_map/ppermute | solution.py:46
  57.6 8.8 %collective-permute-start.12 = (bf16[64,1024]{1,0:T(8,128)(2,1)S(1)}, bf16[64,1024]{1,0:T(8,128)(2,1)S(1)}, u32[]{:S(2)}, u32[]{:S(2)}) collective-permute-start(bf16[64,1024]{1,0:T(8,128)(2,1)S(1)} %add_convert_fusion.1), channel_id=1, source_target_pairs={{0,32},{1,33},{2,34},{3,35},{4,36},{5,37},{6,38},{7,39},{8,40},{9,... | collective-permute-start | bytes 393224 | tf_op jit(solution)/shard_map/ppermute | solution.py:46
  62.0 8.1 %collective-permute-start.20 = (f16[72,1024]{1,0:T(8,128)(2,1)S(1)}, f16[72,1024]{1,0:T(8,128)(2,1)S(1)}, u32[]{:S(2)}, u32[]{:S(2)}) collective-permute-start(f16[72,1024]{1,0:T(8,128)(2,1)S(1)} %pad_maximum_fusion.18), channel_id=1, source_target_pairs={{0,128},{1,129},{2,130},{3,131},{4,132},{5,133},{6,134},{7,135},{8... | collective-permute-start | bytes 442376 | tf_op jit(solution)/shard_map/ppermute | solution.py:46
  70.3 6.5 %collective-permute-start.23 = (bf16[64,1024]{1,0:T(8,128)(2,1)S(1)}, bf16[64,1024]{1,0:T(8,128)(2,1)S(1)}, u32[]{:S(2)}, u32[]{:S(2)}) collective-permute-start(bf16[64,1024]{1,0:T(8,128)(2,1)S(1)} %add_convert_fusion), channel_id=1, source_target_pairs={{0,96},{1,97},{2,98},{3,99},{4,100},{5,101},{6,102},{7,103},{8,104... | collective-permute-start | bytes 393224 | tf_op jit(solution)/shard_map/ppermute | solution.py:46
  70.4 6.4 %collective-permute-start.22 = (bf16[64,1024]{1,0:T(8,128)(2,1)S(1)}, bf16[64,1024]{1,0:T(8,128)(2,1)S(1)}, u32[]{:S(2)}, u32[]{:S(2)}) collective-permute-start(bf16[64,1024]{1,0:T(8,128)(2,1)S(1)} %add_convert_fusion), channel_id=1, source_target_pairs={{0,64},{1,65},{2,66},{3,67},{4,68},{5,69},{6,70},{7,71},{8,72},{9,... | collective-permute-start | bytes 393224 | tf_op jit(solution)/shard_map/ppermute | solution.py:46
  73.7 11.0 %collective-permute-start.16 = (f16[136,1536]{1,0:T(8,128)(2,1)S(1)}, f16[136,1536]{1,0:T(8,128)(2,1)S(1)}, u32[]{:S(2)}, u32[]{:S(2)}) collective-permute-start(f16[136,1536]{1,0:T(8,128)(2,1)S(1)} %pad_maximum_fusion.7), channel_id=1, source_target_pairs={{0,4},{1,5},{2,6},{3,7},{4,0},{5,1},{6,2},{7,3},{8,12},{9,13},{10,... | collective-permute-start | bytes 1253384 | tf_op jit(solution)/shard_map/ppermute | solution.py:46
  79.2 19.1 %collective-permute-start.25 = (f16[136,1536]{1,0:T(8,128)(2,1)S(1)}, f16[136,1536]{1,0:T(8,128)(2,1)S(1)}, u32[]{:S(2)}, u32[]{:S(2)}) collective-permute-start(f16[136,1536]{1,0:T(8,128)(2,1)S(1)} %get-tuple-element.82), channel_id=1, source_target_pairs={{0,8},{1,9},{2,10},{3,11},{4,12},{5,13},{6,14},{7,15},{8,0},{9,1},... | collective-permute-start | bytes 1253384 | tf_op jit(solution)/shard_map/ppermute | solution.py:46
  84.7 13.6 %collective-permute-start.24 = (f16[136,1536]{1,0:T(8,128)(2,1)S(1)}, f16[136,1536]{1,0:T(8,128)(2,1)S(1)}, u32[]{:S(2)}, u32[]{:S(2)}) collective-permute-start(f16[136,1536]{1,0:T(8,128)(2,1)S(1)} %get-tuple-element.81), channel_id=1, source_target_pairs={{0,12},{1,13},{2,14},{3,15},{4,8},{5,9},{6,10},{7,11},{8,4},{9,5},... | collective-permute-start | bytes 1253384 | tf_op jit(solution)/shard_map/ppermute | solution.py:46
  99.0 5.6 %collective-permute-start.27 = (f16[40,1536]{1,0:T(8,128)(2,1)S(1)}, f16[40,1536]{1,0:T(8,128)(2,1)S(1)}, u32[]{:S(2)}, u32[]{:S(2)}) collective-permute-start(f16[40,1536]{1,0:T(8,128)(2,1)S(1)} %get-tuple-element.79), channel_id=1, source_target_pairs={{0,2},{1,3},{2,0},{3,1},{4,6},{5,7},{6,4},{7,5},{8,10},{9,11},{10,... | collective-permute-start | bytes 368648 | tf_op jit(solution)/shard_map/ppermute | solution.py:46
  (8 other events, 42.5 us)
